TPU v7x, 128 devices: a whole 4x4x4 slice. The times are simulated.
128 devices in a mesh: dp: 32 (over x_hi, y, z), tensor: 4 (over x_lo, core).
Axes of the slice: x: 4 (x_hi: 2, x_lo: 2; x = x_hi * 2 + x_lo), y: 4, z: 4, core: 2. Of those that a mesh axis runs over, the one named last changes fastest.
Arguments:
- tokens: bfloat16 [1024, 8192], P('dp', 'tensor'), may hold values from -6 to 6
- out_grad: bfloat16 [1024, 8192], P('dp', 'tensor'), may hold values from -6 to 6
- gate_weight: bfloat16 [8192, 28672], P('tensor', 'dp'), may hold values from -0.0625 to 0.0625
- up_weight: bfloat16 [8192, 28672], P('tensor', 'dp'), may hold values from -0.0625 to 0.0625
- down_weight: bfloat16 [28672, 8192], P('dp', 'tensor'), may hold values from -0.0625 to 0.0625
- pocket_ids: int32 [1024], replicated, may hold values from 0 to 15, never falling along the last dimension, each value on 1 to 341 neighbouring positions
Outputs:
- act_cov: float32 [8192, 8192], P('tensor', 'dp')
- grad_cov: float32 [8192, 8192], P('tensor', 'dp')
- hidden_cov: float32 [28672, 1024], P(('dp', 'tensor'))
- gate_grad_cov: float32 [28672, 1024], P(('dp', 'tensor'))
- up_grad_cov: float32 [28672, 1024], P(('dp', 'tensor'))
Inputs may be any that keep to these rules, and one draw needn't show every extreme that they name: `pocket_ids`: pocket ids never fall along the tokens, every one of the 16 pockets holds at least one token and at most 341, and one holds exactly 341.
All inputs are finite; a program needn't handle non-finite values.
Results may differ from a plain program's by a relative error of at most 0.0043.
Values may be sent and summed in bfloat16 or wider, within the bound.
A program may use at most 192 MiB of HBM per device.

v0:
```python
import jax
import jax.numpy as jnp
from jax import lax
from jax.sharding import PartitionSpec as P

BLOCK = 1024
POCKETS = 16


def spread(array, axis, root):
    mine = lax.axis_index(axis) == root
    return lax.psum(jnp.where(mine, array, jnp.zeros_like(array)), axis)


def from_behind(block, axis, distance):
    devices = range(lax.axis_size(axis))
    route = [(i - distance, i) for i in devices if i - distance in devices]
    return lax.ppermute(block, axis, route)


def pocket_weights(pocket_ids):
    membership = (pocket_ids[:, None] == jnp.arange(POCKETS, dtype=jnp.int32)[None, :]).astype(
        jnp.float32
    )
    counts = jnp.sum(membership, axis=0)
    pocket_share = 1.0 / (POCKETS * counts)
    return jnp.sum(membership * pocket_share[None, :], axis=1)


def local(tokens, out_grad, gate_weight, up_weight, down_weight, pocket_ids):
    rows_all, grads_all = (
        lax.all_gather(tokens, "dp", axis=0, tiled=True),
        lax.all_gather(out_grad, "dp", axis=0, tiled=True),
    )
    weights = pocket_weights(pocket_ids)
    n_tensor = lax.axis_size("tensor")
    n_dp = lax.axis_size("dp")
    units_dp = gate_weight.shape[1]
    unit_count = units_dp // n_tensor
    gate_part = lax.dot_general(
        gate_weight, rows_all, (((0,), (1,)), ((), ())), preferred_element_type=jnp.float32
    )
    up_part = lax.dot_general(
        up_weight, rows_all, (((0,), (1,)), ((), ())), preferred_element_type=jnp.float32
    )
    forward = lax.psum_scatter(
        jnp.stack([gate_part, up_part], axis=1), "tensor", scatter_dimension=0, tiled=True
    )
    gate_t = forward[:, 0, :]
    up_t = forward[:, 1, :]
    back_t = lax.psum_scatter(
        lax.dot_general(
            down_weight, grads_all, (((1,), (1,)), ((), ())), preferred_element_type=jnp.float32
        ),
        "tensor",
        scatter_dimension=0,
        tiled=True,
    )
    col_width = gate_weight.shape[0] * n_tensor // n_dp
    dp_index = lax.axis_index("dp")
    per_tensor = n_dp // n_tensor
    owner_root = dp_index // per_tensor
    col_offset = dp_index % per_tensor * col_width
    token_cols = lax.dynamic_slice_in_dim(rows_all, col_offset, col_width, 1)
    grad_cols = lax.dynamic_slice_in_dim(grads_all, col_offset, col_width, 1)
    token_cols, grad_cols = (
        spread(token_cols, "tensor", owner_root),
        spread(grad_cols, "tensor", owner_root),
    )
    scaled_rows = (rows_all * weights[:, None]).astype(jnp.bfloat16)
    scaled_grads = (grads_all * weights[:, None]).astype(jnp.bfloat16)
    act_cov = lax.dot_general(
        scaled_rows, token_cols, (((0,), (0,)), ((), ())), preferred_element_type=jnp.float32
    )
    grad_cov = lax.dot_general(
        scaled_grads, grad_cols, (((0,), (0,)), ((), ())), preferred_element_type=jnp.float32
    )
    sigmoid_gate = jax.nn.sigmoid(gate_t)
    activated = gate_t * sigmoid_gate
    hidden_t = (activated * up_t).astype(jnp.bfloat16)
    gate_grad_t = (back_t * up_t * sigmoid_gate * (1.0 + gate_t * (1.0 - sigmoid_gate))).astype(
        jnp.bfloat16
    )
    up_grad_t = (back_t * activated).astype(jnp.bfloat16)
    stacked = jnp.stack([hidden_t, gate_grad_t, up_grad_t])
    scaled = (stacked * weights[None, None, :]).astype(jnp.bfloat16)
    own_start = lax.axis_index(("dp", "tensor")) * unit_count
    pieces = []
    reach_units = (unit_count + BLOCK - 2) // unit_count
    for offset in range(-reach_units, reach_units + 1):
        if offset == 0:
            pieces.append(stacked)
        else:
            pieces.append(from_behind(stacked, ("dp", "tensor"), -offset))
    window_start = own_start - reach_units * unit_count
    window_rows = jnp.concatenate(pieces, axis=1)

    def block_product(column_start):
        block_cols = lax.dynamic_slice_in_dim(window_rows, column_start - window_start, BLOCK, 1)
        return jnp.einsum("kit,kjt->kij", scaled, block_cols, preferred_element_type=jnp.float32)

    first_start = own_start // BLOCK * BLOCK
    edge_start = first_start + BLOCK
    row_global = own_start + jnp.arange(unit_count, dtype=jnp.int32)

    def single_block():
        return block_product(first_start)

    def split_blocks():
        lower = block_product(first_start)
        upper = block_product(edge_start)
        below = (row_global < edge_start)[None, :, None]
        return jnp.where(below, lower, upper)

    blockwise = lax.cond(own_start + unit_count > edge_start, split_blocks, single_block)
    return (act_cov, grad_cov, blockwise[0], blockwise[1], blockwise[2])


def solution(mesh):
    return jax.shard_map(
        local,
        mesh=mesh,
        in_specs=(
            P("dp", "tensor"),
            P("dp", "tensor"),
            P("tensor", "dp"),
            P("tensor", "dp"),
            P("dp", "tensor"),
            P(),
        ),
        out_specs=(
            P("tensor", "dp"),
            P("tensor", "dp"),
            P(("dp", "tensor"), None),
            P(("dp", "tensor"), None),
            P(("dp", "tensor"), None),
        ),
        check_vma=False,
    )
```

profile of v0, /device:TPU:90, one launch (start us, length us, event | category | flops | bytes accessed | tf_op | source)
XLA Modules:
  0.0 590.5 jit_solution(3284610645114607825)
XLA Ops:
  7.2 0.7 all-gather.5.cloned.1.call-update
  7.9 0.7 all-gather.3.cloned.1.call-update
  8.7 83.1 %all-gather.5.cloned.1.call-done = bf16[1024,2048]{1,0:T(8,128)(2,1)} async-done(((bf16[32,2048]{1,0:T(8,128)(2,1)}), bf16[1024,2048]{1,0:T(8,128)(2,1)}) %all-gather.5.cloned.1.call-update) | async-done | bytes 4194320 | tf_op jit(solution)/shard_map/all_gather | solution.py:33
  91.7 9.1 %fusion.33 = f32[896,1024]{1,0:T(8,128)} fusion(bf16[896,2048]{1,0:T(8,128)(2,1)} %param.12, bf16[1024,2048]{1,0:T(8,128)(2,1)} %all-gather.5.cloned.1.call-done), kind=kOutput, calls=%fused_computation.68 | convolution fusion | flops 3758096384 | bytes 11534336 | tf_op jit(solution)/shard_map/dot_general | solution.py:52
  100.9 73.3 %all-gather.3.cloned.1.call-done = bf16[1024,2048]{1,0:T(8,128)(2,1)} async-done(((bf16[32,2048]{1,0:T(8,128)(2,1)}), bf16[1024,2048]{1,0:T(8,128)(2,1)}) %all-gather.3.cloned.1.call-update) | async-done | bytes 4194320 | tf_op jit(solution)/shard_map/all_gather | solution.py:32
  174.2 7.1 %convolution_bitcast_fusion = f32[896,1,1024]{2,0,1:T(8,128)S(1)} fusion(bf16[2048,896]{1,0:T(8,128)(2,1)} %param.11, bf16[1024,2048]{1,0:T(8,128)(2,1)} %all-gather.3.cloned.1.call-done), kind=kOutput, calls=%fused_computation.26 | convolution fusion | flops 3758096384 | bytes 11534336 | tf_op jit(solution)/shard_map/dot_general | solution.py:43
  181.3 4.0 convolution_bitcast_fusion.1
  185.3 4.3 pad_maximum_fusion
  189.7 1.9 dynamic-slice_select_fusion.1
  191.7 1.9 dynamic-slice_select_fusion
  193.7 23.2 %reduce-scatter.5.cloned.1.call-done = f32[224,1024]{1,0:T(8,128)} async-done(((f32[896,1024]{1,0:T(8,128)}), f32[224,1024]{1,0:T(8,128)}) %reduce-scatter.5.cloned.1.call-update) | async-done | bytes 917520 | tf_op jit(solution)/shard_map/reduce_scatter | solution.py:51
  216.9 74.3 %reduce-scatter.3.cloned.1.call-done = f32[224,2,1024]{2,0,1:T(8,128)} async-done(((f32[896,2,1024]{2,0,1:T(8,128)}), f32[224,2,1024]{2,0,1:T(8,128)}) %reduce-scatter.3.cloned.1.call-update) | async-done | bytes 1835024 | tf_op jit(solution)/shard_map/reduce_scatter | solution.py:46
  291.2 2.4 fusion.32
  293.9 1.2 pad_maximum_fusion.1
  295.2 2.9 collective-permute-start
  298.0 4.0 collective-permute-start.1
  302.0 4.7 collective-permute-start.2
  306.7 4.3 collective-permute-start.3
  311.1 1.9 collective-permute-start.4
  313.1 40.1 %all-reduce.3.cloned.1.call-done = (bf16[1024,256]{1,0:T(8,128)(2,1)}, bf16[1024,256]{1,0:T(8,128)(2,1)}) async-done(((bf16[1024,256]{1,0:T(8,128)(2,1)}, bf16[1024,256]{1,0:T(8,128)(2,1)}), (bf16[1024,256]{1,0:T(8,128)(2,1)}, bf16[1024,256]{1,0:T(8,128)(2,1)})) %all-reduce.3.cloned.1.call-update) | async-done | bytes 1048592 | tf_op jit(solution)/shard_map/psum | solution.py:12
  353.2 5.4 fusion.14
  358.6 45.6 %collective-permute-start.5 = (bf16[3,224,1024]{2,1,0:T(8,128)(2,1)}, bf16[3,224,1024]{2,1,0:T(8,128)(2,1)S(1)}, u32[]{:S(2)}, u32[]{:S(2)}) collective-permute-start(bf16[3,224,1024]{2,1,0:T(8,128)(2,1)} %pad_maximum_fusion.1), channel_id=1, source_target_pairs={{1,0},{2,1},{3,2},{4,3},{5,4},{6,5},{7,6},{8,7},{9,8},{10,9},{11,1... | collective-permute-start | bytes 4128776 | tf_op jit(solution)/shard_map/ppermute | solution.py:18
  404.2 30.2 %collective-permute-start.6 = (bf16[3,224,1024]{2,1,0:T(8,128)(2,1)}, bf16[3,224,1024]{2,1,0:T(8,128)(2,1)S(1)}, u32[]{:S(2)}, u32[]{:S(2)}) collective-permute-start(bf16[3,224,1024]{2,1,0:T(8,128)(2,1)} %pad_maximum_fusion.1), channel_id=1, source_target_pairs={{2,0},{3,1},{4,2},{5,3},{6,4},{7,5},{8,6},{9,7},{10,8},{11,9},{12,... | collective-permute-start | bytes 4128776 | tf_op jit(solution)/shard_map/ppermute | solution.py:18
  434.4 3.2 fusion.15
  437.6 2.0 collective-permute-start.7
  439.7 2.3 collective-permute-start.8
  442.0 0.3 multiply_convert_fusion.4
  442.3 7.3 %collective-permute-start.9 = (bf16[3,224,1024]{2,1,0:T(8,128)(2,1)}, bf16[3,224,1024]{2,1,0:T(8,128)(2,1)S(1)}, u32[]{:S(2)}, u32[]{:S(2)}) collective-permute-start(bf16[3,224,1024]{2,1,0:T(8,128)(2,1)} %pad_maximum_fusion.1), channel_id=1, source_target_pairs={{5,0},{6,1},{7,2},{8,3},{9,4},{10,5},{11,6},{12,7},{13,8},{14,9},{... | collective-permute-start | bytes 4128776 | tf_op jit(solution)/shard_map/ppermute | solution.py:18
  449.6 1.3 constant_dynamic-update-slice_fusion.10
  450.9 2.5 constant_dynamic-update-slice_fusion.9
  453.4 2.6 constant_dynamic-update-slice_fusion.8
  456.0 2.5 constant_dynamic-update-slice_fusion.7
  458.5 2.5 constant_dynamic-update-slice_fusion.6
  461.1 1.2 constant_dynamic-update-slice_fusion.5
  462.3 1.3 constant_dynamic-update-slice_fusion.4
  463.6 63.6 %collective-permute-done.6 = bf16[3,224,1024]{2,1,0:T(8,128)(2,1)S(1)} collective-permute-done((bf16[3,224,1024]{2,1,0:T(8,128)(2,1)}, bf16[3,224,1024]{2,1,0:T(8,128)(2,1)S(1)}, u32[]{:S(2)}, u32[]{:S(2)}) %collective-permute-start.6) | collective-permute-done | bytes 1376288 | tf_op jit(solution)/shard_map/ppermute | solution.py:18
  527.1 1.2 constant_dynamic-update-slice_fusion.3
  528.3 5.2 collective-permute-done.7
  533.5 1.2 constant_dynamic-update-slice_fusion.2
  534.7 38.7 %collective-permute-done.8 = bf16[3,224,1024]{2,1,0:T(8,128)(2,1)S(1)} collective-permute-done((bf16[3,224,1024]{2,1,0:T(8,128)(2,1)}, bf16[3,224,1024]{2,1,0:T(8,128)(2,1)S(1)}, u32[]{:S(2)}, u32[]{:S(2)}) %collective-permute-start.8) | collective-permute-done | bytes 1376288 | tf_op jit(solution)/shard_map/ppermute | solution.py:18
  573.5 1.2 constant_dynamic-update-slice_fusion.1
  574.7 1.5 collective-permute-done.9
  576.2 1.2 constant_dynamic-update-slice_fusion
  577.4 5.0 conditional.1
  577.4 4.8 fusion.2
  582.5 0.9 copy-done.3
  583.4 0.3 copy-done.4
  583.7 0.3 copy-done.5
  (39 shorter events, 1.0 us)
Async XLA Ops:
  7.2 84.6 %all-gather.5.cloned.1.call-start = ((), (), s32[]{:S(2)}) async-start(), calls=%async_computation.3 | async-start | bytes 4325376 | tf_op jit(solution)/shard_map/all_gather | solution.py:33
  7.9 166.3 %all-gather.3.cloned.1.call-start = ((), (), s32[]{:S(2)}) async-start(), calls=%async_computation.2 | async-start | bytes 4325376 | tf_op jit(solution)/shard_map/all_gather | solution.py:32
  8.6 208.2 %reduce-scatter.5.cloned.1.call-start = ((), (), s32[]{:S(2)}) async-start(), calls=%async_computation.5 | async-start | bytes 4587520 | tf_op jit(solution)/shard_map/reduce_scatter | solution.py:51
  100.9 190.3 %reduce-scatter.3.cloned.1.call-start = ((), (), s32[]{:S(2)}) async-start(), calls=%async_computation.4 | async-start | bytes 9175040 | tf_op jit(solution)/shard_map/reduce_scatter | solution.py:46
  174.2 7.1 %copy-start.7 = (bf16[1024,2048]{1,0:T(8,128)(2,1)S(1)}, bf16[1024,2048]{1,0:T(8,128)(2,1)}, u32[]{:S(2)}) copy-start(bf16[1024,2048]{1,0:T(8,128)(2,1)} %all-gather.3.cloned.1.call-done) | copy-start | bytes 12582916
  174.2 7.1 %copy-start.9 = (bf16[2048,896]{1,0:T(8,128)(2,1)S(1)}, bf16[2048,896]{1,0:T(8,128)(2,1)}, u32[]{:S(2)}) copy-start(bf16[2048,896]{1,0:T(8,128)(2,1)} %param.10) | copy-start | bytes 11010052
  189.7 163.5 %all-reduce.3.cloned.1.call-start = ((), (), s32[]{:S(2)}) async-start(), calls=%async_computation.6 | async-start | bytes 2097152 | tf_op jit(solution)/shard_map/psum | solution.py:12
  193.6 117.3 %copy-start.8 = (s32[1024]{0:T(1024)S(1)}, s32[1024]{0:T(1024)}, u32[]{:S(2)}) copy-start(s32[1024]{0:T(1024)} %param.13) | copy-start | bytes 12292
  291.2 2.5 copy-start
  295.2 63.5 %collective-permute-start = (bf16[3,224,1024]{2,1,0:T(8,128)(2,1)}, bf16[3,224,1024]{2,1,0:T(8,128)(2,1)S(1)}, u32[]{:S(2)}, u32[]{:S(2)}) collective-permute-start(bf16[3,224,1024]{2,1,0:T(8,128)(2,1)} %pad_maximum_fusion.1), channel_id=1, source_target_pairs={{0,5},{1,6},{2,7},{3,8},{4,9},{5,10},{6,11},{7,12},{8,13},{9,14},{... | collective-permute-start | bytes 4128776 | tf_op jit(solution)/shard_map/ppermute | solution.py:18
  298.0 106.2 %collective-permute-start.1 = (bf16[3,224,1024]{2,1,0:T(8,128)(2,1)}, bf16[3,224,1024]{2,1,0:T(8,128)(2,1)}, u32[]{:S(2)}, u32[]{:S(2)}) collective-permute-start(bf16[3,224,1024]{2,1,0:T(8,128)(2,1)} %pad_maximum_fusion.1), channel_id=1, source_target_pairs={{0,4},{1,5},{2,6},{3,7},{4,8},{5,9},{6,10},{7,11},{8,12},{9,13},{1... | collective-permute-start | bytes 4128776 | tf_op jit(solution)/shard_map/ppermute | solution.py:18
  302.0 135.6 %collective-permute-start.2 = (bf16[3,224,1024]{2,1,0:T(8,128)(2,1)}, bf16[3,224,1024]{2,1,0:T(8,128)(2,1)}, u32[]{:S(2)}, u32[]{:S(2)}) collective-permute-start(bf16[3,224,1024]{2,1,0:T(8,128)(2,1)} %pad_maximum_fusion.1), channel_id=1, source_target_pairs={{0,3},{1,4},{2,5},{3,6},{4,7},{5,8},{6,9},{7,10},{8,11},{9,12},{10... | collective-permute-start | bytes 4128776 | tf_op jit(solution)/shard_map/ppermute | solution.py:18
  306.7 133.0 %collective-permute-start.3 = (bf16[3,224,1024]{2,1,0:T(8,128)(2,1)}, bf16[3,224,1024]{2,1,0:T(8,128)(2,1)}, u32[]{:S(2)}, u32[]{:S(2)}) collective-permute-start(bf16[3,224,1024]{2,1,0:T(8,128)(2,1)} %pad_maximum_fusion.1), channel_id=1, source_target_pairs={{0,2},{1,3},{2,4},{3,5},{4,6},{5,7},{6,8},{7,9},{8,10},{9,11},{10,... | collective-permute-start | bytes 4128776 | tf_op jit(solution)/shard_map/ppermute | solution.py:18
  311.1 131.2 %collective-permute-start.4 = (bf16[3,224,1024]{2,1,0:T(8,128)(2,1)}, bf16[3,224,1024]{2,1,0:T(8,128)(2,1)}, u32[]{:S(2)}, u32[]{:S(2)}) collective-permute-start(bf16[3,224,1024]{2,1,0:T(8,128)(2,1)} %pad_maximum_fusion.1), channel_id=1, source_target_pairs={{0,1},{1,2},{2,3},{3,4},{4,5},{5,6},{6,7},{7,8},{8,9},{9,10},{10,1... | collective-permute-start | bytes 4128776 | tf_op jit(solution)/shard_map/ppermute | solution.py:18
  353.2 81.2 %copy-start.6 = (bf16[1024,2048]{1,0:T(8,128)(2,1)S(1)}, bf16[1024,2048]{1,0:T(8,128)(2,1)}, u32[]{:S(2)}) copy-start(bf16[1024,2048]{1,0:T(8,128)(2,1)} %all-gather.5.cloned.1.call-done) | copy-start | bytes 12582916
  353.2 81.2 %copy-start.10 = (bf16[1024,256]{1,0:T(8,128)(2,1)S(1)}, bf16[1024,256]{1,0:T(8,128)(2,1)}, u32[]{:S(2)}) copy-start(bf16[1024,256]{1,0:T(8,128)(2,1)} %get-tuple-element.71) | copy-start | bytes 1572868
  358.6 79.0 %copy-start.1 = (bf16[3,224,1024]{2,1,0:T(8,128)(2,1)}, bf16[3,224,1024]{2,1,0:T(8,128)(2,1)S(1)}, u32[]{:S(2)}) copy-start(bf16[3,224,1024]{2,1,0:T(8,128)(2,1)S(1)} %collective-permute-done) | copy-start | bytes 4128772
  358.6 103.7 %collective-permute-start.5 = (bf16[3,224,1024]{2,1,0:T(8,128)(2,1)}, bf16[3,224,1024]{2,1,0:T(8,128)(2,1)S(1)}, u32[]{:S(2)}, u32[]{:S(2)}) collective-permute-start(bf16[3,224,1024]{2,1,0:T(8,128)(2,1)} %pad_maximum_fusion.1), channel_id=1, source_target_pairs={{1,0},{2,1},{3,2},{4,3},{5,4},{6,5},{7,6},{8,7},{9,8},{10,9},{11,1... | collective-permute-start | bytes 4128776 | tf_op jit(solution)/shard_map/ppermute | solution.py:18
  404.2 122.9 %collective-permute-start.6 = (bf16[3,224,1024]{2,1,0:T(8,128)(2,1)}, bf16[3,224,1024]{2,1,0:T(8,128)(2,1)S(1)}, u32[]{:S(2)}, u32[]{:S(2)}) collective-permute-start(bf16[3,224,1024]{2,1,0:T(8,128)(2,1)} %pad_maximum_fusion.1), channel_id=1, source_target_pairs={{2,0},{3,1},{4,2},{5,3},{6,4},{7,5},{8,6},{9,7},{10,8},{11,9},{12,... | collective-permute-start | bytes 4128776 | tf_op jit(solution)/shard_map/ppermute | solution.py:18
  437.6 12.0 %copy-start.2 = (bf16[3,224,1024]{2,1,0:T(8,128)(2,1)S(1)}, bf16[3,224,1024]{2,1,0:T(8,128)(2,1)}, u32[]{:S(2)}) copy-start(bf16[3,224,1024]{2,1,0:T(8,128)(2,1)} %copy-done.1) | copy-start | bytes 4128772
  437.6 95.9 %collective-permute-start.7 = (bf16[3,224,1024]{2,1,0:T(8,128)(2,1)}, bf16[3,224,1024]{2,1,0:T(8,128)(2,1)S(1)}, u32[]{:S(2)}, u32[]{:S(2)}) collective-permute-start(bf16[3,224,1024]{2,1,0:T(8,128)(2,1)} %pad_maximum_fusion.1), channel_id=1, source_target_pairs={{3,0},{4,1},{5,2},{6,3},{7,4},{8,5},{9,6},{10,7},{11,8},{12,9},{13... | collective-permute-start | bytes 4128776 | tf_op jit(solution)/shard_map/ppermute | solution.py:18
  439.7 133.8 %collective-permute-start.8 = (bf16[3,224,1024]{2,1,0:T(8,128)(2,1)}, bf16[3,224,1024]{2,1,0:T(8,128)(2,1)S(1)}, u32[]{:S(2)}, u32[]{:S(2)}) collective-permute-start(bf16[3,224,1024]{2,1,0:T(8,128)(2,1)} %pad_maximum_fusion.1), channel_id=1, source_target_pairs={{4,0},{5,1},{6,2},{7,3},{8,4},{9,5},{10,6},{11,7},{12,8},{13,9},{1... | collective-permute-start | bytes 4128776 | tf_op jit(solution)/shard_map/ppermute | solution.py:18
  442.3 133.9 %collective-permute-start.9 = (bf16[3,224,1024]{2,1,0:T(8,128)(2,1)}, bf16[3,224,1024]{2,1,0:T(8,128)(2,1)S(1)}, u32[]{:S(2)}, u32[]{:S(2)}) collective-permute-start(bf16[3,224,1024]{2,1,0:T(8,128)(2,1)} %pad_maximum_fusion.1), channel_id=1, source_target_pairs={{5,0},{6,1},{7,2},{8,3},{9,4},{10,5},{11,6},{12,7},{13,8},{14,9},{... | collective-permute-start | bytes 4128776 | tf_op jit(solution)/shard_map/ppermute | solution.py:18
  582.4 0.9 copy-start.3
  582.5 1.2 copy-start.4
  582.5 1.5 copy-start.5
Sparse Core Ops, SparseCore 0:
  11.1 80.5 all-gather.4
  94.9 79.2 all-gather.2
  176.6 40.1 reduce-scatter.4
  219.1 72.0 reduce-scatter.2
  294.2 58.9 all-reduce.2
where the time goes:
time: 591 us; the launch traced here: 590 us
  waiting for transfers between devices  404 us (68%)
  starting transfers between devices  105 us (18%)
  matrix products  33.6 us (6%)
  local copies, waits for them, and re-layouts  19.2 us (3%)
  between operations  14.1 us (2%)
  other arithmetic  13.9 us (2%)
    ppermute x10, waiting for transfers between devices, from_behind(): return lax.ppermute(block, axis, route)  109 us
    ppermute x10, starting transfers between devices, from_behind(): return lax.ppermute(block, axis, route)  105 us
    all_gather x1, waiting for transfers between devices, local(): lax.all_gather(out_grad, 'dp', axis=0, tiled=True)  83.1 us
    reduce_scatter x1, waiting for transfers between devices, local(): lax.psum_scatter(jnp.stack([gate_part, up_part], axis=1), 'tensor', scatt...  74.3 us
    all_gather x1, waiting for transfers between devices, local(): lax.all_gather(tokens, 'dp', axis=0, tiled=True)  73.3 us
    psum x1, waiting for transfers between devices, spread(): return lax.psum(jnp.where(mine, array, jnp.zeros_like(array)), axis)  40.1 us
    reduce_scatter x1, waiting for transfers between devices, local(): lax.psum_scatter(lax.dot_general(down_weight, grads_all, (((1,), (1,)), (...  23.2 us
    unnamed x31, local copies, waits for them, and re-layouts  17.9 us
  transfers between devices with their start and end apart: 15, of which 9 were waited for; matrix products, arithmetic and copies ran while one was open for 10% of the time, Pallas kernels for 0%

commit v1 on v0

v1 whole, which is shorter than its diff:
```python
import functools

import jax
import jax.numpy as jnp
from jax import lax
from jax.experimental import pallas as pl
from jax.experimental.pallas import tpu as pltpu
from jax.sharding import PartitionSpec as P

MESH = pl.DeviceIdType.MESH
POCKETS = 16
BF = jnp.bfloat16
F32 = jnp.float32
MIB = 1 << 20
CHUNKS = 4
UNITS = 224
SLICE = 896
PIECE = 128
GATE, UP, BACK = 0, 1, 2
LEVELS = 32767.0
TINY = 1e-30


def mod4(v):
    return lax.rem(v + 4, 4)


class Sems:
    def __init__(self, ref):
        self.ref, self.used = ref, 0

    def take(self, count=1):
        base = self.used
        self.used += count
        return base


def kernel(
    tok, grd, gate_h, up_h, down_h, ids_ref,
    act_o, grad_o, hid_o, gg_o, ug_o,
    xt, wg, wu, wd, pbuf, rbuf, xsend, xrecv, tsend, trecv, vw, sb, cols, wrow, wcol,
    ssem, rsem, lsem,
):
    dp = lax.axis_index("dp")
    tensor = lax.axis_index("tensor")
    xh, y, z = dp // 16, (dp // 4) % 4, dp % 4
    xl, c = tensor // 2, tensor % 2
    e = dp % 8

    def dev(xh_, y_, z_, xl_, c_):
        return {"dp": xh_ * 16 + y_ * 4 + z_, "tensor": xl_ * 2 + c_}

    sibling = dev(xh, y, z, xl, 1 - c)
    partner = dev(xh, y, z, 1 - xl, c)
    twin = dev(1 - xh, y, z, xl, c)
    y_peer = [dev(xh, mod4(y + s), z, xl, c) for s in (1, 2, 3)]
    z_peer = [dev(xh, y, mod4(z + s), xl, c) for s in (1, 2, 3)]
    above = {"dp": lax.rem(dp + 1, 32), "tensor": tensor}
    below = {"dp": lax.rem(dp + 31, 32), "tensor": tensor}
    across = [dev(1 - xh, y, z, 1 - xl, k) for k in (0, 1)]

    send, recv, here = Sems(ssem), Sems(rsem), Sems(lsem)
    unsent = []

    def push(src, dst, to, r=None):
        s = send.take()
        r = recv.take() if r is None else r
        copy = pltpu.make_async_remote_copy(
            src_ref=src, dst_ref=dst, send_sem=ssem.at[s], recv_sem=rsem.at[r],
            device_id=to, device_id_type=MESH,
        )
        copy.start()
        unsent.append(copy.wait_send)
        return r

    def arrived(ref, r):
        pltpu.make_async_copy(ref, ref, rsem.at[r]).wait()

    def stay(src, dst):
        copy = pltpu.make_async_copy(src, dst, lsem.at[here.take()])
        copy.start()
        return copy

    shard = (tok, grd)
    pkg_of = (y, 4 + z)
    inner = (xh * 64 + z * 16, xh * 64 + y * 16)
    twin_inner = ((1 - xh) * 64 + z * 16, (1 - xh) * 64 + y * 16)

    def rows16(ref, a, half, start):
        return ref.at[a, pkg_of[half], pl.ds(pl.multiple_of(start, 16), 16)]

    own_copies = [
        [stay(shard[a].at[pl.ds(16 * h, 16)], rows16(xt, a, h, inner[h])) for h in (0, 1)]
        for a in (0, 1)
    ]
    weight_copies = [stay(gate_h, wg), stay(up_h, wu), stay(down_h, wd)]

    barrier = pltpu.get_barrier_semaphore()
    greeted = [sibling, partner, twin, *y_peer, *z_peer, above, below, *across]
    for peer in greeted:
        pl.semaphore_signal(barrier, inc=1, device_id=peer, device_id_type=MESH)
    pl.semaphore_wait(barrier, len(greeted))

    twin_sem = [[recv.take() for _ in (0, 1)] for _ in (0, 1)]
    ring_sem = [[recv.take() for _ in (0, 1)] for _ in (0, 1)]
    ring_peer = (z_peer, y_peer)
    def start_twin(a):
        for h in (0, 1):
            push(shard[a].at[pl.ds(16 * h, 16)], rows16(xt, a, h, inner[h]), twin, twin_sem[a][h])

    def start_ring(a):
        for h in (0, 1):
            for peer in ring_peer[h]:
                push(shard[a].at[pl.ds(16 * h, 16)], rows16(xt, a, h, inner[h]), peer, ring_sem[a][h])

    def forward_twin(a):
        for h in (0, 1):
            piece = rows16(xt, a, h, twin_inner[h])
            arrived(piece, twin_sem[a][h])
            for peer in ring_peer[h]:
                push(piece, piece, peer, ring_sem[a][h])

    side_peer = ((y_peer[2], y_peer[0]), (z_peer[2], z_peer[0]))
    side_sem = [[[recv.take() for _ in (0, 1)] for _ in (0, 1)] for _ in (0, 1)]
    far_sem = [[[recv.take() for _ in (0, 1)] for _ in (0, 1)] for _ in (0, 1)]
    coord = (y, z)

    def package(h, step):
        return 4 * h + mod4(coord[h] + step)

    def send_packages(a):
        for h in (0, 1):
            own_copies[a][h].wait()
            arrived(xt.at[a, pkg_of[h], pl.ds(0, 96)], ring_sem[a][h])
            whole = xt.at[a, pkg_of[h]]
            for s in (0, 1):
                push(whole, whole, side_peer[h][s], side_sem[a][h][1 - s])

    def forward_packages(a):
        for h in (0, 1):
            for s in (0, 1):
                whole = xt.at[a, package(h, (-1, 1)[s])]
                arrived(whole, side_sem[a][h][s])
                part = xt.at[a, package(h, (-1, 1)[s]), pl.ds(64 * s, 64)]
                push(part, part, side_peer[h][1 - s], far_sem[a][h][s])

    def far_packages(a):
        for h in (0, 1):
            for s in (0, 1):
                arrived(xt.at[a, package(h, 2), pl.ds(64 * s, 64)], far_sem[a][h][s])

    chunk_pkgs = [
        (package(0, 0), package(1, 0)),
        (package(0, -1), package(0, 1)),
        (package(1, -1), package(1, 1)),
        (package(0, 2), package(1, 2)),
    ]

    def pkgs_of(k, y_, z_):
        return [
            (y_, 4 + z_),
            (mod4(y_ - 1), mod4(y_ + 1)),
            (4 + mod4(z_ - 1), 4 + mod4(z_ + 1)),
            (mod4(y_ + 2), 4 + mod4(z_ + 2)),
        ][k]

    core_sem = [[recv.take() for _ in range(3)] for _ in range(CHUNKS)]
    line_sem = [[recv.take() for _ in range(3)] for _ in range(CHUNKS)]
    top_sem = [[recv.take() for _ in range(3)] for _ in range(CHUNKS)]
    slot_of = {}
    slot_sent = [None] * 3
    weights_in = [False] * 3

    def project(k, m):
        if not weights_in[m]:
            weight_copies[m].wait()
            weights_in[m] = True
        slot = len(slot_of) % 3
        assert (k, m, slot) not in slot_of and not any(v == slot for v in busy.values())
        a = 1 if m == BACK else 0
        x = jnp.concatenate([xt[a, chunk_pkgs[k][0]], xt[a, chunk_pkgs[k][1]]], axis=0)
        if m == BACK:
            part = lax.dot_general(wd[...], x, (((1,), (1,)), ((), ())), preferred_element_type=F32)
        else:
            w = (wg, wu)[m]
            part = lax.dot_general(w[...], x, (((0,), (1,)), ((), ())), preferred_element_type=F32)
        if slot_sent[slot] is not None:
            slot_sent[slot]()
        for i in range(4):
            pbuf[slot, i // 2, i % 2] = part[UNITS * i : UNITS * (i + 1)]
        push(pbuf.at[slot, :, 1 - c], rbuf.at[k, m], sibling, core_sem[k][m])
        slot_sent[slot] = unsent.pop()
        slot_of[k, m] = slot
        busy[k, m] = slot

    busy = {}

    def combine(k, m):
        slot = busy.pop((k, m))
        arrived(rbuf.at[k, m], core_sem[k][m])

        def add(i, top):
            r = pl.ds(pl.multiple_of(i * 32, 32), 32)
            value = rbuf[k, m, 1 - xl, r] + pbuf[slot, 1 - xl, c, r]
            rbuf[k, m, 1 - xl, r] = value
            rbuf[k, m, xl, r] = rbuf[k, m, xl, r] + pbuf[slot, xl, c, r]
            return jnp.maximum(top, jnp.abs(value))

        top = lax.fori_loop(0, UNITS // 32, add, jnp.zeros((32, 256), F32))
        top = jnp.max(top, axis=0, keepdims=True)
        tsend[k, m] = top
        scale = jnp.where(top > TINY, 1.0 / jnp.maximum(top, TINY), 0.0)

        def code(i, _):
            r = pl.ds(pl.multiple_of(i * 32, 32), 32)
            value = rbuf[k, m, 1 - xl, r]
            share = jnp.abs(value) * scale
            root = share * lax.rsqrt(jnp.maximum(share, TINY))
            level = (root * LEVELS + 0.5).astype(jnp.int32)
            xsend[k, m, r] = jnp.where(value < 0, -level, level).astype(jnp.int16)
            return 0

        lax.fori_loop(0, UNITS // 32, code, 0)
        push(tsend.at[k, m], trecv.at[k, m], partner, top_sem[k][m])
        push(xsend.at[k, m], xrecv.at[k, m], partner, line_sem[k][m])

    base = 1024 - PIECE * e

    def rows_of(t):
        return pl.ds(pl.multiple_of(base + UNITS * t, 32), UNITS)

    part_of = (pl.ds(0, 1), pl.ds(1, 2))
    own_sem, cross_sem, relay_sem = (
        [[[recv.take() for _ in (0, 1)] for _ in (0, 1)] for _ in range(CHUNKS)] for _ in range(3)
    )

    def units(part, k, q, t):
        return vw.at[part_of[part], chunk_pkgs[k][q], rows_of(t)]

    def finish(k, part):
        for m in (GATE, UP) if part == 0 else (BACK,):
            arrived(trecv.at[k, m], top_sem[k][m])
            arrived(xrecv.at[k, m], line_sem[k][m])

        def total(m, r):
            root = xrecv[k, m, r].astype(F32) * (1.0 / LEVELS)
            return rbuf[k, m, xl, r] + root * jnp.abs(root) * trecv[k, m]

        def body(i, _):
            r = pl.ds(pl.multiple_of(i * 32, 32), 32)
            gate, up = total(GATE, r), total(UP, r)
            sig = 1.0 / (1.0 + jnp.exp(-gate))
            activated = gate * sig
            if part == 0:
                values = ((0, activated * up),)
            else:
                back = total(BACK, r)
                values = ((1, back * up * sig * (1.0 + gate * (1.0 - sig))), (2, back * activated))
            wr = pl.ds(pl.multiple_of(base + UNITS * tensor + i * 32, 32), 32)
            for j, value in values:
                value = value.astype(BF)
                for q in (0, 1):
                    p = chunk_pkgs[k][q]
                    v = value[:, 128 * q : 128 * (q + 1)]
                    vw[j, p, wr] = v
                    sb[j, p, r] = (v.astype(F32) * wrow[p]).astype(BF)
            return 0

        lax.fori_loop(0, UNITS // 32, body, 0)
        for q in (0, 1):
            mine = units(part, k, q, tensor)
            push(mine, mine, partner, cross_sem[k][part][q])
            push(mine, mine, sibling, own_sem[k][part][q])

    def relay(k, part):
        for q in (0, 1):
            theirs = units(part, k, q, (1 - xl) * 2 + c)
            arrived(theirs, cross_sem[k][part][q])
            push(theirs, theirs, sibling, relay_sem[k][part][q])

    def slice_complete(k):
        for part in (0, 1):
            for q in (0, 1):
                arrived(units(part, k, q, xl * 2 + 1 - c), own_sem[k][part][q])
                arrived(units(part, k, q, (1 - xl) * 2 + 1 - c), relay_sem[k][part][q])

    first = xl == 0
    n_down = jnp.where(jnp.logical_or(jnp.logical_not(first), e <= 4), e, 0)
    n_up = jnp.where(jnp.logical_or(first, e >= 3), 7 - e, 0)
    n_from_above = jnp.where(jnp.logical_or(e <= 3, jnp.logical_and(jnp.logical_not(first), e <= 6)), e + 1, 0)
    n_from_below = jnp.where(jnp.logical_or(e >= 4, jnp.logical_and(first, e >= 1)), 8 - e, 0)
    down_sem = [(send.take(7), recv.take(7)) for _ in range(CHUNKS)]
    up_sem = [(send.take(7), recv.take(7)) for _ in range(CHUNKS)]
    down_relay = [(send.take(7), recv.take(7)) for _ in range(CHUNKS)]
    up_relay = [(send.take(7), recv.take(7)) for _ in range(CHUNKS)]
    dp_above, dp_below = dp + 1, dp + 31
    my_pkg = [jnp.where(c == 0, *chunk_pkgs[k]) for k in range(CHUNKS)]
    above_yz = ((dp_above // 4) % 4, dp_above % 4)
    below_yz = ((dp_below // 4) % 4, dp_below % 4)

    def win(p, row):
        return vw.at[:, p, pl.ds(pl.multiple_of(row, PIECE), PIECE)]

    def down_copy(k, j):
        s, r = down_sem[k]
        return pltpu.make_async_remote_copy(
            src_ref=win(my_pkg[k], base + PIECE * j),
            dst_ref=win(my_pkg[k], base + 1024 + PIECE * j),
            send_sem=ssem.at[s + j], recv_sem=rsem.at[r + j],
            device_id=below, device_id_type=MESH,
        )

    def up_copy(k, i):
        s, r = up_sem[k]
        return pltpu.make_async_remote_copy(
            src_ref=win(my_pkg[k], base + PIECE * (e + i)),
            dst_ref=win(my_pkg[k], PIECE * i),
            send_sem=ssem.at[s + i], recv_sem=rsem.at[r + i],
            device_id=above, device_id_type=MESH,
        )

    def loop(n, f):
        def body(j, _):
            f(j)
            return 0

        lax.fori_loop(0, n, body, 0)

    def send_neighbours(k):
        loop(n_down, lambda j: down_copy(k, j).start())
        loop(n_up, lambda j: up_copy(k, j).start())

    def from_above(k, q, j):
        p = jnp.where(q == 0, *pkgs_of(k, *above_yz))
        return win(p, base + SLICE + PIECE * j)

    def from_below(k, q, i):
        p = jnp.where(q == 0, *pkgs_of(k, *below_yz))
        return win(p, PIECE * i)

    def pass_on(ref, sems, j):
        return pltpu.make_async_remote_copy(
            src_ref=ref, dst_ref=ref, send_sem=ssem.at[sems[0] + j], recv_sem=rsem.at[sems[1] + j],
            device_id=sibling, device_id_type=MESH,
        )

    def relay_neighbours(k):
        def one_above(j):
            ref = from_above(k, c, j)
            pltpu.make_async_copy(ref, ref, rsem.at[down_sem[k][1] + j]).wait()
            pass_on(ref, down_relay[k], j).start()

        def one_below(i):
            ref = from_below(k, c, i)
            pltpu.make_async_copy(ref, ref, rsem.at[up_sem[k][1] + i]).wait()
            pass_on(ref, up_relay[k], i).start()

        loop(n_from_above, one_above)
        loop(n_from_below, one_below)

    def neighbours_complete(k):
        def one_above(j):
            ref = from_above(k, 1 - c, j)
            pltpu.make_async_copy(ref, ref, rsem.at[down_relay[k][1] + j]).wait()

        def one_below(i):
            ref = from_below(k, 1 - c, i)
            pltpu.make_async_copy(ref, ref, rsem.at[up_relay[k][1] + i]).wait()

        loop(n_from_above, one_above)
        loop(n_from_below, one_below)

    def neighbours_sent(k):
        loop(n_down, lambda j: down_copy(k, j).wait_send())
        loop(n_up, lambda j: up_copy(k, j).wait_send())
        loop(n_from_above, lambda j: pass_on(from_above(k, c, j), down_relay[k], j).wait_send())
        loop(n_from_below, lambda i: pass_on(from_below(k, c, i), up_relay[k], i).wait_send())

    col_sem = [recv.take() for _ in (0, 1)]
    col_send = [send.take(2) for _ in (0, 1)]
    col_here = [here.take() for _ in (0, 1)]
    holder = c == y // 2
    at_home = xl == xh
    col_start = pl.multiple_of(e * 256, 256)

    def col_copies(a):
        src = xt.at[a, :, :, pl.ds(col_start, 256)]
        make = lambda to, i: pltpu.make_async_remote_copy(
            src_ref=src, dst_ref=cols.at[a], send_sem=ssem.at[col_send[a] + i], recv_sem=rsem.at[col_sem[a]],
            device_id=to, device_id_type=MESH,
        )
        return make(sibling, 0), make(across[0], 0), make(across[1], 1), pltpu.make_async_copy(
            src, cols.at[a], lsem.at[col_here[a]]
        )

    home_holder = jnp.logical_and(holder, at_home)
    far_holder = jnp.logical_and(holder, jnp.logical_not(at_home))

    def send_cols(a):
        home, far0, far1, local = col_copies(a)

        @pl.when(home_holder)
        def _():
            home.start()
            local.start()

        @pl.when(far_holder)
        def _():
            far0.start()
            far1.start()

    def cols_complete(a):
        _, _, _, local = col_copies(a)

        @pl.when(home_holder)
        def _():
            local.wait()

        @pl.when(jnp.logical_not(home_holder))
        def _():
            arrived(cols.at[a], col_sem[a])

    def cols_sent(a):
        home, far0, far1, _ = col_copies(a)

        @pl.when(home_holder)
        def _():
            home.wait_send()

        @pl.when(far_holder)
        def _():
            far0.wait_send()
            far1.wait_send()

    cov_out = (act_o, grad_o)

    def full_cov(a):
        rhs = cols[a].reshape(1024, 256)

        def body(i, _):
            k = pl.ds(pl.multiple_of(i * 256, 256), 256)
            parts = [
                (xt[a, p, :, k].astype(F32) * wcol[:, p : p + 1]).astype(BF) for p in range(8)
            ]
            cov_out[a][k] = lax.dot_general(
                jnp.concatenate(parts, axis=0), rhs, (((0,), (0,)), ((), ())), preferred_element_type=F32
            )
            return 0

        lax.fori_loop(0, 8, body, 0)

    split_row = PIECE * e - UNITS * tensor
    blk_out = (hid_o, gg_o, ug_o)

    def block_cov(j):
        def body(i, _):
            k = pl.multiple_of(i * 256, 256)
            lhs = jnp.concatenate([sb[j, p] for p in range(8)], axis=1)

            def product(start):
                rhs = jnp.concatenate([vw[j, p, pl.ds(start + k, 256)] for p in range(8)], axis=1)
                return lax.dot_general(lhs, rhs, (((1,), (1,)), ((), ())), preferred_element_type=F32)

            @pl.when(split_row < UNITS)
            def _():
                blk_out[j][:, pl.ds(k, 256)] = product(1024)

            @pl.when(split_row > 0)
            def _():
                row = lax.broadcasted_iota(jnp.int32, (UNITS, 256), 0)
                blk_out[j][:, pl.ds(k, 256)] = jnp.where(
                    row < split_row, product(0), blk_out[j][:, pl.ds(k, 256)]
                )

            return 0

        lax.fori_loop(0, 4, body, 0)

    def pocket_weights():
        ids = ids_ref[...]
        weights = jnp.zeros((8, 128), F32)
        for k in range(POCKETS):
            member = (ids == k).astype(F32)
            count = jnp.sum(jnp.sum(member, axis=1, keepdims=True), axis=0, keepdims=True)
            weights = weights + member * (1.0 / (POCKETS * count))
        for p in range(8):
            wrow[p] = weights[p : p + 1]
        wcol[...] = weights.T

    start_twin(0)
    start_twin(1)
    start_ring(0)
    pocket_weights()
    forward_twin(0)
    start_ring(1)
    forward_twin(1)
    send_packages(0)
    project(0, GATE)
    project(0, UP)
    combine(0, GATE)
    send_packages(1)
    project(0, BACK)
    combine(0, UP)
    combine(0, BACK)
    finish(0, 0)
    forward_packages(0)
    project(1, GATE)
    project(1, UP)
    combine(1, GATE)
    project(2, GATE)
    combine(1, UP)
    project(2, UP)
    combine(2, GATE)
    combine(2, UP)
    finish(0, 1)
    forward_packages(1)
    project(1, BACK)
    project(2, BACK)
    combine(1, BACK)
    combine(2, BACK)
    finish(1, 0)
    finish(2, 0)
    relay(0, 0)
    relay(0, 1)
    far_packages(0)
    send_cols(0)
    project(3, GATE)
    project(3, UP)
    combine(3, GATE)
    combine(3, UP)
    slice_complete(0)
    send_neighbours(0)
    finish(1, 1)
    finish(2, 1)
    far_packages(1)
    send_cols(1)
    project(3, BACK)
    combine(3, BACK)
    finish(3, 0)
    for k in (1, 2):
        relay(k, 0)
    for k in (1, 2):
        relay(k, 1)
        slice_complete(k)
        send_neighbours(k)
    relay_neighbours(0)
    finish(3, 1)
    cols_complete(0)
    full_cov(0)
    relay(3, 0)
    relay(3, 1)
    slice_complete(3)
    send_neighbours(3)
    relay_neighbours(1)
    cols_complete(1)
    full_cov(1)
    relay_neighbours(2)
    relay_neighbours(3)
    for k in range(CHUNKS):
        neighbours_complete(k)
    for j in range(3):
        block_cov(j)
    for wait in slot_sent + unsent:
        wait()
    for k in range(CHUNKS):
        neighbours_sent(k)
    for a in (0, 1):
        cols_sent(a)


N_SEND, N_RECV, N_LOCAL = 380, 320, 24


def local(tokens, out_grad, gate_weight, up_weight, down_weight, pocket_ids):
    ids = pocket_ids.reshape(2, 4, 4, 2, 16)
    ids = jnp.concatenate(
        [
            ids[:, :, :, 0].transpose(1, 0, 2, 3).reshape(4, 128),
            ids[:, :, :, 1].transpose(2, 0, 1, 3).reshape(4, 128),
        ]
    )
    any_spec = pl.BlockSpec(memory_space=pl.ANY)
    vmem = pl.BlockSpec(memory_space=pltpu.VMEM)
    return pl.pallas_call(
        kernel,
        out_shape=[
            pltpu.VMEM((2048, 256), F32),
            pltpu.VMEM((2048, 256), F32),
            pltpu.VMEM((UNITS, 1024), F32),
            pltpu.VMEM((UNITS, 1024), F32),
            pltpu.VMEM((UNITS, 1024), F32),
        ],
        in_specs=[any_spec] * 5 + [vmem],
        out_specs=[vmem] * 5,
        scratch_shapes=[
            pltpu.VMEM((2, 8, 128, 2048), BF),
            pltpu.VMEM((2048, SLICE), BF),
            pltpu.VMEM((2048, SLICE), BF),
            pltpu.VMEM((SLICE, 2048), BF),
            pltpu.VMEM((3, 2, 2, UNITS, 256), F32),
            pltpu.VMEM((CHUNKS, 3, 2, UNITS, 256), F32),
            pltpu.VMEM((CHUNKS, 3, UNITS, 256), jnp.int16),
            pltpu.VMEM((CHUNKS, 3, UNITS, 256), jnp.int16),
            pltpu.VMEM((CHUNKS, 3, 1, 256), F32),
            pltpu.VMEM((CHUNKS, 3, 1, 256), F32),
            pltpu.VMEM((3, 8, 2048, 128), BF),
            pltpu.VMEM((3, 8, UNITS, 128), BF),
            pltpu.VMEM((2, 8, 128, 256), BF),
            pltpu.VMEM((8, 1, 128), F32),
            pltpu.VMEM((128, 8), F32),
            pltpu.SemaphoreType.DMA((N_SEND,)),
            pltpu.SemaphoreType.DMA((N_RECV,)),
            pltpu.SemaphoreType.DMA((N_LOCAL,)),
        ],
        compiler_params=pltpu.CompilerParams(
            collective_id=0, has_side_effects=True, vmem_limit_bytes=52 * MIB
        ),
        name="ekfac_factors",
    )(tokens, out_grad, gate_weight, up_weight, down_weight, ids)


def solution(mesh):
    return jax.shard_map(
        local,
        mesh=mesh,
        in_specs=(
            P("dp", "tensor"),
            P("dp", "tensor"),
            P("tensor", "dp"),
            P("tensor", "dp"),
            P("dp", "tensor"),
            P(),
        ),
        out_specs=(
            P("tensor", "dp"),
            P("tensor", "dp"),
            P(("dp", "tensor"), None),
            P(("dp", "tensor"), None),
            P(("dp", "tensor"), None),
        ),
        check_vma=False,
    )
```

time: 591 us -> 146 us (0.25)
  the two profiles are of different devices: /device:TPU:90 before, /device:TPU:32 now
where the time goes in v1:
time: 146 us
  Pallas kernels  138 us (95%)
  local copies, waits for them, and re-layouts  6.4 us (4%)
    pallas_call x1, Pallas kernels, local(): pl.pallas_call(kernel, out_shape=[pltpu.VMEM((2048, 256), F32), pltpu.VME...  138 us
    unnamed x5, local copies, waits for them, and re-layouts  5.41 us

profile of v1, /device:TPU:32, one launch (start us, length us, event | category | flops | bytes accessed | tf_op | source)
XLA Modules:
  0.0 145.9 jit_solution(1931104629977703433)
XLA Ops:
  0.6 0.8 reshape.19
  1.5 0.1 reshape.20
  1.6 0.1 reshape.21
  1.7 0.6 pad_add_fusion.ids_ref
  2.3 138.2 %ekfac_factors.1 = (f32[2048,256]{1,0:T(8,128)S(1)}, f32[2048,256]{1,0:T(8,128)S(1)}, f32[224,1024]{1,0:T(8,128)S(1)}, f32[224,1024]{1,0:T(8,128)S(1)}, f32[224,1024]{1,0:T(8,128)S(1)}) custom-call(bf16[32,2048]{1,0:T(8,128)(2,1)} %tok.1, bf16[32,2048]{1,0:T(8,128)(2,1)} %grd.1, bf16[2048,896]{1,0:T(8,128)(2,1)} %gate_h.1, bf16[2048,896]{1,0:T(8,128)(2,1)} %up_h.1, ...), custom_call_target="tpu_custom_call" | custom-call | tf_op jit(solution)/shard_map/ekfac_factors/pallas_call | solution.py:584
  140.5 1.3 copy.19
  141.8 0.9 copy.21
  142.7 0.9 copy.22
  143.7 0.9 copy.23
  144.6 1.3 copy.20
  (3 shorter events, 0.0 us)

commit v2 on v1

--- a/solution.py
+++ b/solution.py
@@ -38,7 +38,7 @@
 def kernel(
     tok, grd, gate_h, up_h, down_h, ids_ref,
     act_o, grad_o, hid_o, gg_o, ug_o,
-    xt, wg, wu, wd, pbuf, rbuf, xsend, xrecv, tsend, trecv, vw, sb, cols, wrow, wcol,
+    xt, wg, wu, wd, pbuf, rbuf, xsend, xrecv, tsend, trecv, vw, sb, cols, stage, res, wrow, wcol,
     ssem, rsem, lsem,
 ):
     dp = lax.axis_index("dp")
@@ -55,23 +55,26 @@
     twin = dev(1 - xh, y, z, xl, c)
     y_peer = [dev(xh, mod4(y + s), z, xl, c) for s in (1, 2, 3)]
     z_peer = [dev(xh, y, mod4(z + s), xl, c) for s in (1, 2, 3)]
-    above = {"dp": lax.rem(dp + 1, 32), "tensor": tensor}
-    below = {"dp": lax.rem(dp + 31, 32), "tensor": tensor}
+    around = [{"dp": lax.rem(dp + s, 32), "tensor": t} for s in (1, 31) for t in range(4)]
+    above, below = ({"dp": lax.rem(dp + s, 32), "tensor": tensor} for s in (1, 31))
     across = [dev(1 - xh, y, z, 1 - xl, k) for k in (0, 1)]
 
     send, recv, here = Sems(ssem), Sems(rsem), Sems(lsem)
-    unsent = []
-
-    def push(src, dst, to, r=None):
-        s = send.take()
-        r = recv.take() if r is None else r
+    groups = {}
+
+    def push(src, dst, to, r, group):
+        s = groups.setdefault(group, None)
+        if s is None:
+            s = groups[group] = send.take()
         copy = pltpu.make_async_remote_copy(
             src_ref=src, dst_ref=dst, send_sem=ssem.at[s], recv_sem=rsem.at[r],
             device_id=to, device_id_type=MESH,
         )
         copy.start()
-        unsent.append(copy.wait_send)
-        return r
+        return copy
+
+    def group_sent(group, ref):
+        pltpu.make_async_copy(ref, ref, ssem.at[groups.pop(group)]).wait()
 
     def arrived(ref, r):
         pltpu.make_async_copy(ref, ref, rsem.at[r]).wait()
@@ -95,8 +98,21 @@
     ]
     weight_copies = [stay(gate_h, wg), stay(up_h, wu), stay(down_h, wd)]
 
+    def pocket_weights():
+        ids = ids_ref[...]
+        weights = jnp.zeros((8, 128), F32)
+        for k in range(POCKETS):
+            member = (ids == k).astype(F32)
+            count = jnp.sum(jnp.sum(member, axis=1, keepdims=True), axis=0, keepdims=True)
+            weights = weights + member * (1.0 / (POCKETS * count))
+        for p in range(8):
+            wrow[p] = weights[p : p + 1]
+        wcol[...] = weights.T
+
+    pocket_weights()
+
     barrier = pltpu.get_barrier_semaphore()
-    greeted = [sibling, partner, twin, *y_peer, *z_peer, above, below, *across]
+    greeted = [sibling, partner, twin, *y_peer, *z_peer, *across, *around]
     for peer in greeted:
         pl.semaphore_signal(barrier, inc=1, device_id=peer, device_id_type=MESH)
     pl.semaphore_wait(barrier, len(greeted))
@@ -106,19 +122,19 @@
     ring_peer = (z_peer, y_peer)
     def start_twin(a):
         for h in (0, 1):
-            push(shard[a].at[pl.ds(16 * h, 16)], rows16(xt, a, h, inner[h]), twin, twin_sem[a][h])
+            push(shard[a].at[pl.ds(16 * h, 16)], rows16(xt, a, h, inner[h]), twin, twin_sem[a][h], "twin")
 
     def start_ring(a):
         for h in (0, 1):
             for peer in ring_peer[h]:
-                push(shard[a].at[pl.ds(16 * h, 16)], rows16(xt, a, h, inner[h]), peer, ring_sem[a][h])
+                push(shard[a].at[pl.ds(16 * h, 16)], rows16(xt, a, h, inner[h]), peer, ring_sem[a][h], "ring")
 
     def forward_twin(a):
         for h in (0, 1):
             piece = rows16(xt, a, h, twin_inner[h])
             arrived(piece, twin_sem[a][h])
             for peer in ring_peer[h]:
-                push(piece, piece, peer, ring_sem[a][h])
+                push(piece, piece, peer, ring_sem[a][h], "ring")
 
     side_peer = ((y_peer[2], y_peer[0]), (z_peer[2], z_peer[0]))
     side_sem = [[[recv.take() for _ in (0, 1)] for _ in (0, 1)] for _ in (0, 1)]
@@ -134,7 +150,7 @@
             arrived(xt.at[a, pkg_of[h], pl.ds(0, 96)], ring_sem[a][h])
             whole = xt.at[a, pkg_of[h]]
             for s in (0, 1):
-                push(whole, whole, side_peer[h][s], side_sem[a][h][1 - s])
+                push(whole, whole, side_peer[h][s], side_sem[a][h][1 - s], "side")
 
     def forward_packages(a):
         for h in (0, 1):
@@ -142,7 +158,7 @@
                 whole = xt.at[a, package(h, (-1, 1)[s])]
                 arrived(whole, side_sem[a][h][s])
                 part = xt.at[a, package(h, (-1, 1)[s]), pl.ds(64 * s, 64)]
-                push(part, part, side_peer[h][1 - s], far_sem[a][h][s])
+                push(part, part, side_peer[h][1 - s], far_sem[a][h][s], "far")
 
     def far_packages(a):
         for h in (0, 1):
@@ -176,7 +192,7 @@
             weight_copies[m].wait()
             weights_in[m] = True
         slot = len(slot_of) % 3
-        assert (k, m, slot) not in slot_of and not any(v == slot for v in busy.values())
+        assert slot not in busy.values()
         a = 1 if m == BACK else 0
         x = jnp.concatenate([xt[a, chunk_pkgs[k][0]], xt[a, chunk_pkgs[k][1]]], axis=0)
         if m == BACK:
@@ -185,11 +201,10 @@
             w = (wg, wu)[m]
             part = lax.dot_general(w[...], x, (((0,), (1,)), ((), ())), preferred_element_type=F32)
         if slot_sent[slot] is not None:
-            slot_sent[slot]()
+            slot_sent[slot].wait_send()
         for i in range(4):
             pbuf[slot, i // 2, i % 2] = part[UNITS * i : UNITS * (i + 1)]
-        push(pbuf.at[slot, :, 1 - c], rbuf.at[k, m], sibling, core_sem[k][m])
-        slot_sent[slot] = unsent.pop()
+        slot_sent[slot] = push(pbuf.at[slot, :, 1 - c], rbuf.at[k, m], sibling, core_sem[k][m], slot)
         slot_of[k, m] = slot
         busy[k, m] = slot
 
@@ -221,8 +236,8 @@
             return 0
 
         lax.fori_loop(0, UNITS // 32, code, 0)
-        push(tsend.at[k, m], trecv.at[k, m], partner, top_sem[k][m])
-        push(xsend.at[k, m], xrecv.at[k, m], partner, line_sem[k][m])
+        push(tsend.at[k, m], trecv.at[k, m], partner, top_sem[k][m], "top")
+        push(xsend.at[k, m], xrecv.at[k, m], partner, line_sem[k][m], "line")
 
     base = 1024 - PIECE * e
 
@@ -231,11 +246,14 @@
 
     part_of = (pl.ds(0, 1), pl.ds(1, 2))
     own_sem, cross_sem, relay_sem = (
-        [[[recv.take() for _ in (0, 1)] for _ in (0, 1)] for _ in range(CHUNKS)] for _ in range(3)
+        [[recv.take() for _ in (0, 1)] for _ in range(CHUNKS)] for _ in range(3)
     )
 
     def units(part, k, q, t):
         return vw.at[part_of[part], chunk_pkgs[k][q], rows_of(t)]
+
+    def units_arrived(part, t, r):
+        arrived(vw.at[part_of[part], pl.ds(0, 2), rows_of(t)], r)
 
     def finish(k, part):
         for m in (GATE, UP) if part == 0 else (BACK,):
@@ -269,112 +287,140 @@
         lax.fori_loop(0, UNITS // 32, body, 0)
         for q in (0, 1):
             mine = units(part, k, q, tensor)
-            push(mine, mine, partner, cross_sem[k][part][q])
-            push(mine, mine, sibling, own_sem[k][part][q])
+            push(mine, mine, partner, cross_sem[k][part], "cross")
+        for q in (0, 1):
+            mine = units(part, k, q, tensor)
+            push(mine, mine, sibling, own_sem[k][part], "own")
 
     def relay(k, part):
+        units_arrived(part, (1 - xl) * 2 + c, cross_sem[k][part])
         for q in (0, 1):
             theirs = units(part, k, q, (1 - xl) * 2 + c)
-            arrived(theirs, cross_sem[k][part][q])
-            push(theirs, theirs, sibling, relay_sem[k][part][q])
+            push(theirs, theirs, sibling, relay_sem[k][part], "relay")
 
     def slice_complete(k):
         for part in (0, 1):
-            for q in (0, 1):
-                arrived(units(part, k, q, xl * 2 + 1 - c), own_sem[k][part][q])
-                arrived(units(part, k, q, (1 - xl) * 2 + 1 - c), relay_sem[k][part][q])
-
-    first = xl == 0
-    n_down = jnp.where(jnp.logical_or(jnp.logical_not(first), e <= 4), e, 0)
-    n_up = jnp.where(jnp.logical_or(first, e >= 3), 7 - e, 0)
-    n_from_above = jnp.where(jnp.logical_or(e <= 3, jnp.logical_and(jnp.logical_not(first), e <= 6)), e + 1, 0)
-    n_from_below = jnp.where(jnp.logical_or(e >= 4, jnp.logical_and(first, e >= 1)), 8 - e, 0)
-    down_sem = [(send.take(7), recv.take(7)) for _ in range(CHUNKS)]
-    up_sem = [(send.take(7), recv.take(7)) for _ in range(CHUNKS)]
-    down_relay = [(send.take(7), recv.take(7)) for _ in range(CHUNKS)]
-    up_relay = [(send.take(7), recv.take(7)) for _ in range(CHUNKS)]
-    dp_above, dp_below = dp + 1, dp + 31
+            units_arrived(part, xl * 2 + 1 - c, own_sem[k][part])
+            units_arrived(part, (1 - xl) * 2 + 1 - c, relay_sem[k][part])
+
+    low = e <= 3
+    n_down = jnp.where(e <= 4, e, 0)
+    n_up = jnp.where(jnp.logical_and(e >= 3, e <= 6), 7 - e, 0)
+    n_near = jnp.where(low, e + 1, 8 - e)
+    near_row = jnp.where(low, base + SLICE, 0)
+    near_dp = jnp.where(low, dp + 1, dp + 31)
+    near_y, near_z = (near_dp // 4) % 4, near_dp % 4
     my_pkg = [jnp.where(c == 0, *chunk_pkgs[k]) for k in range(CHUNKS)]
-    above_yz = ((dp_above // 4) % 4, dp_above % 4)
-    below_yz = ((dp_below // 4) % 4, dp_below % 4)
-
-    def win(p, row):
-        return vw.at[:, p, pl.ds(pl.multiple_of(row, PIECE), PIECE)]
-
-    def down_copy(k, j):
-        s, r = down_sem[k]
+    near_pkg = [jnp.where(c == 0, *pkgs_of(k, near_y, near_z)) for k in range(CHUNKS)]
+    near_sem, near_relay = ([recv.take() for _ in range(CHUNKS)] for _ in range(2))
+    down_send, up_send, near_send = ([send.take() for _ in range(CHUNKS)] for _ in range(3))
+
+    def sized(count, most, f):
+        for n in range(1, most + 1):
+            pl.when(count == n)(functools.partial(f, n))
+
+    def win(p, row, n):
+        return vw.at[:, p, pl.ds(pl.multiple_of(row, PIECE), n * PIECE)]
+
+    def down_copy(k, n):
         return pltpu.make_async_remote_copy(
-            src_ref=win(my_pkg[k], base + PIECE * j),
-            dst_ref=win(my_pkg[k], base + 1024 + PIECE * j),
-            send_sem=ssem.at[s + j], recv_sem=rsem.at[r + j],
+            src_ref=win(my_pkg[k], base, n), dst_ref=win(my_pkg[k], base + 1024, n),
+            send_sem=ssem.at[down_send[k]], recv_sem=rsem.at[near_sem[k]],
             device_id=below, device_id_type=MESH,
         )
 
-    def up_copy(k, i):
-        s, r = up_sem[k]
+    def up_copy(k, n):
         return pltpu.make_async_remote_copy(
-            src_ref=win(my_pkg[k], base + PIECE * (e + i)),
-            dst_ref=win(my_pkg[k], PIECE * i),
-            send_sem=ssem.at[s + i], recv_sem=rsem.at[r + i],
+            src_ref=win(my_pkg[k], base + PIECE * e, n), dst_ref=win(my_pkg[k], 0, n),
+            send_sem=ssem.at[up_send[k]], recv_sem=rsem.at[near_sem[k]],
             device_id=above, device_id_type=MESH,
         )
 
-    def loop(n, f):
-        def body(j, _):
-            f(j)
-            return 0
-
-        lax.fori_loop(0, n, body, 0)
-
-    def send_neighbours(k):
-        loop(n_down, lambda j: down_copy(k, j).start())
-        loop(n_up, lambda j: up_copy(k, j).start())
-
-    def from_above(k, q, j):
-        p = jnp.where(q == 0, *pkgs_of(k, *above_yz))
-        return win(p, base + SLICE + PIECE * j)
-
-    def from_below(k, q, i):
-        p = jnp.where(q == 0, *pkgs_of(k, *below_yz))
-        return win(p, PIECE * i)
-
-    def pass_on(ref, sems, j):
+    def near_copy(k, n):
+        ref = win(near_pkg[k], near_row, n)
         return pltpu.make_async_remote_copy(
-            src_ref=ref, dst_ref=ref, send_sem=ssem.at[sems[0] + j], recv_sem=rsem.at[sems[1] + j],
+            src_ref=ref, dst_ref=ref, send_sem=ssem.at[near_send[k]], recv_sem=rsem.at[near_relay[k]],
             device_id=sibling, device_id_type=MESH,
         )
 
+    def send_neighbours(k):
+        sized(n_down, 4, lambda n: down_copy(k, n).start())
+        sized(n_up, 4, lambda n: up_copy(k, n).start())
+
     def relay_neighbours(k):
-        def one_above(j):
-            ref = from_above(k, c, j)
-            pltpu.make_async_copy(ref, ref, rsem.at[down_sem[k][1] + j]).wait()
-            pass_on(ref, down_relay[k], j).start()
-
-        def one_below(i):
-            ref = from_below(k, c, i)
-            pltpu.make_async_copy(ref, ref, rsem.at[up_sem[k][1] + i]).wait()
-            pass_on(ref, up_relay[k], i).start()
-
-        loop(n_from_above, one_above)
-        loop(n_from_below, one_below)
+        def go(n):
+            arrived(win(near_pkg[k], near_row, n), near_sem[k])
+            near_copy(k, n).start()
+
+        sized(n_near, 4, go)
 
     def neighbours_complete(k):
-        def one_above(j):
-            ref = from_above(k, 1 - c, j)
-            pltpu.make_async_copy(ref, ref, rsem.at[down_relay[k][1] + j]).wait()
-
-        def one_below(i):
-            ref = from_below(k, 1 - c, i)
-            pltpu.make_async_copy(ref, ref, rsem.at[up_relay[k][1] + i]).wait()
-
-        loop(n_from_above, one_above)
-        loop(n_from_below, one_below)
+        sized(n_near, 4, lambda n: arrived(win(near_pkg[k], near_row, n), near_relay[k]))
 
     def neighbours_sent(k):
-        loop(n_down, lambda j: down_copy(k, j).wait_send())
-        loop(n_up, lambda j: up_copy(k, j).wait_send())
-        loop(n_from_above, lambda j: pass_on(from_above(k, c, j), down_relay[k], j).wait_send())
-        loop(n_from_below, lambda i: pass_on(from_below(k, c, i), up_relay[k], i).wait_send())
+        sized(n_down, 4, lambda n: down_copy(k, n).wait_send())
+        sized(n_up, 4, lambda n: up_copy(k, n).wait_send())
+        sized(n_near, 4, lambda n: near_copy(k, n).wait_send())
+
+    major = jnp.logical_or(e <= 2, e >= 5)
+    n_cols = jnp.where(low, 7 - e, e)
+    first_col = jnp.where(low, e, 0)
+    res_sem = recv.take(8)
+    res_send = send.take(24)
+    pair = (tensor, tensor + 4)
+
+    def result_copy(i, r, h):
+        row = jnp.where(low, 0, PIECE * (e - 1)) + PIECE * i + 32 * r
+        owner = row // UNITS
+        col = jnp.where(low, 0, 8 - e) + pair[h]
+        return pltpu.make_async_remote_copy(
+            src_ref=stage.at[:, i, pl.ds(32 * r, 32), pl.ds(128 * h, 128)],
+            dst_ref=res.at[
+                :, pl.ds(pl.multiple_of(row - UNITS * owner, 32), 32), pl.ds(pl.multiple_of(128 * col, 128), 128)
+            ],
+            send_sem=ssem.at[res_send + 8 * i + 2 * r + h], recv_sem=rsem.at[res_sem + col],
+            device_id={"dp": near_dp % 32, "tensor": owner}, device_id_type=MESH,
+        )
+
+    def each_result(i, f):
+        for h in (0, 1):
+            @pl.when(pair[h] < n_cols)
+            def _():
+                for r in range(4):
+                    f(result_copy(i, r, h))
+
+    def products_for_neighbour():
+        def body(i, _):
+            rows = pl.ds(pl.multiple_of(near_row + PIECE * i, PIECE), PIECE)
+            cols_at = [
+                pl.ds(pl.multiple_of(base + PIECE * (first_col + jnp.minimum(piece, n_cols - 1)), PIECE), PIECE)
+                for piece in pair
+            ]
+            for j in range(3):
+                lhs = jnp.concatenate(
+                    [(vw[j, p, rows].astype(F32) * wrow[p]).astype(BF) for p in range(8)], axis=1
+                )
+                rhs = jnp.concatenate(
+                    [jnp.concatenate([vw[j, p, at] for at in cols_at], axis=0) for p in range(8)], axis=1
+                )
+                stage[j, i] = lax.dot_general(
+                    lhs, rhs, (((1,), (1,)), ((), ())), preferred_element_type=F32
+                ).astype(BF)
+            each_result(i, lambda copy: copy.start())
+            return 0
+
+        @pl.when(major)
+        def _():
+            lax.fori_loop(0, n_near, body, 0)
+
+    def products_sent():
+        def body(i, _):
+            each_result(i, lambda copy: copy.wait_send())
+            return 0
+
+        @pl.when(major)
+        def _():
+            lax.fori_loop(0, n_near, body, 0)
 
     col_sem = [recv.take() for _ in (0, 1)]
     col_send = [send.take(2) for _ in (0, 1)]
@@ -449,48 +495,62 @@
 
         lax.fori_loop(0, 8, body, 0)
 
-    split_row = PIECE * e - UNITS * tensor
+    split_row = jnp.clip(PIECE * e - UNITS * tensor, 0, UNITS)
+    has_early, has_late = split_row > 0, split_row < UNITS
     blk_out = (hid_o, gg_o, ug_o)
 
-    def block_cov(j):
-        def body(i, _):
-            k = pl.multiple_of(i * 256, 256)
-            lhs = jnp.concatenate([sb[j, p] for p in range(8)], axis=1)
-
-            def product(start):
+    def block_cov():
+        row = lax.broadcasted_iota(jnp.int32, (UNITS, 256), 0)
+
+        def body(g, _):
+            k = pl.multiple_of(g * 256, 256)
+
+            def product(j, start):
+                lhs = jnp.concatenate([sb[j, p] for p in range(8)], axis=1)
                 rhs = jnp.concatenate([vw[j, p, pl.ds(start + k, 256)] for p in range(8)], axis=1)
                 return lax.dot_general(lhs, rhs, (((1,), (1,)), ((), ())), preferred_element_type=F32)
 
-            @pl.when(split_row < UNITS)
+            @pl.when(jnp.logical_and(has_late, jnp.logical_or(low, 2 * g <= 6 - e)))
             def _():
-                blk_out[j][:, pl.ds(k, 256)] = product(1024)
-
-            @pl.when(split_row > 0)
+                for j in range(3):
+                    blk_out[j][:, pl.ds(k, 256)] = product(j, 1024)
+
+            @pl.when(jnp.logical_and(has_early, jnp.logical_or(jnp.logical_not(low), 2 * g + 1 >= 8 - e)))
             def _():
-                row = lax.broadcasted_iota(jnp.int32, (UNITS, 256), 0)
-                blk_out[j][:, pl.ds(k, 256)] = jnp.where(
-                    row < split_row, product(0), blk_out[j][:, pl.ds(k, 256)]
-                )
+                for j in range(3):
+                    blk_out[j][:, pl.ds(k, 256)] = jnp.where(
+                        row < split_row, product(j, 0), blk_out[j][:, pl.ds(k, 256)]
+                    )
 
             return 0
 
         lax.fori_loop(0, 4, body, 0)
 
-    def pocket_weights():
-        ids = ids_ref[...]
-        weights = jnp.zeros((8, 128), F32)
-        for k in range(POCKETS):
-            member = (ids == k).astype(F32)
-            count = jnp.sum(jnp.sum(member, axis=1, keepdims=True), axis=0, keepdims=True)
-            weights = weights + member * (1.0 / (POCKETS * count))
-        for p in range(8):
-            wrow[p] = weights[p : p + 1]
-        wcol[...] = weights.T
+    def products_from_neighbour():
+        row = lax.broadcasted_iota(jnp.int32, (UNITS, 128), 0)
+        minor_early = jnp.logical_and(jnp.logical_and(low, e >= 1), has_early)
+        minor_late = jnp.logical_and(jnp.logical_and(jnp.logical_not(low), e <= 6), has_late)
+        bands = jnp.where(low, split_row, UNITS - split_row) // 32
+        start = jnp.where(low, 0, 7 - e)
+        stop = jnp.where(low, 8 - e, 8)
+        from_row = jnp.where(low, 0, split_row)
+        to_row = jnp.where(low, split_row, UNITS)
+
+        def body(col, _):
+            sized(bands, 7, lambda n: arrived(res.at[:, pl.ds(0, 32 * n), pl.ds(0, 128)], res_sem + col))
+            at = pl.ds(pl.multiple_of(col * 128, 128), 128)
+            here_too = jnp.logical_and(row >= from_row, row < to_row)
+            for j in range(3):
+                blk_out[j][:, at] = jnp.where(here_too, res[j, :, at].astype(F32), blk_out[j][:, at])
+            return 0
+
+        @pl.when(jnp.logical_or(minor_early, minor_late))
+        def _():
+            lax.fori_loop(start, stop, body, 0)
 
     start_twin(0)
+    start_ring(0)
     start_twin(1)
-    start_ring(0)
-    pocket_weights()
     forward_twin(0)
     start_ring(1)
     forward_twin(1)
@@ -558,17 +618,29 @@
     relay_neighbours(3)
     for k in range(CHUNKS):
         neighbours_complete(k)
-    for j in range(3):
-        block_cov(j)
-    for wait in slot_sent + unsent:
-        wait()
+    products_for_neighbour()
+    block_cov()
+    products_from_neighbour()
+    for copy in slot_sent:
+        copy.wait_send()
+    group_sent("twin", xt.at[0, 0, pl.ds(0, 64)])
+    group_sent("ring", xt.at[0, pl.ds(0, 3)])
+    group_sent("side", xt.at[0])
+    group_sent("far", xt.at[0, pl.ds(0, 4)])
+    group_sent("top", tsend)
+    group_sent("line", xsend)
+    group_sent("cross", sb)
+    group_sent("own", sb)
+    group_sent("relay", sb)
     for k in range(CHUNKS):
         neighbours_sent(k)
     for a in (0, 1):
         cols_sent(a)
-
-
-N_SEND, N_RECV, N_LOCAL = 380, 320, 24
+    products_sent()
+    assert (send.used, recv.used, here.used) == (N_SEND, N_RECV, N_LOCAL)
+
+
+N_SEND, N_RECV, N_LOCAL = 52, 102, 9
 
 
 def local(tokens, out_grad, gate_weight, up_weight, down_weight, pocket_ids):
@@ -606,6 +678,8 @@
             pltpu.VMEM((3, 8, 2048, 128), BF),
             pltpu.VMEM((3, 8, UNITS, 128), BF),
             pltpu.VMEM((2, 8, 128, 256), BF),
+            pltpu.VMEM((3, 3, 128, 256), BF),
+            pltpu.VMEM((3, UNITS, 1024), BF),
             pltpu.VMEM((8, 1, 128), F32),
             pltpu.VMEM((128, 8), F32),
             pltpu.SemaphoreType.DMA((N_SEND,)),

time: 146 us -> 130 us (0.89)
  the two profiles are of different devices: /device:TPU:32 before, /device:TPU:15 now
where the time goes in v2:
time: 130 us
  Pallas kernels  122 us (94%)
  local copies, waits for them, and re-layouts  6.4 us (5%)
    pallas_call x1, Pallas kernels, local(): pl.pallas_call(kernel, out_shape=[pltpu.VMEM((2048, 256), F32), pltpu.VME...  122 us
    unnamed x5, local copies, waits for them, and re-layouts  5.41 us

profile of v2, /device:TPU:15, one launch (start us, length us, event | category | flops | bytes accessed | tf_op | source)
XLA Modules:
  0.0 129.5 jit_solution(10907164535657853995)
XLA Ops:
  0.6 0.8 reshape.19
  1.5 0.1 reshape.20
  1.6 0.1 reshape.21
  1.7 0.6 pad_add_fusion.ids_ref
  2.3 121.9 %ekfac_factors.1 = (f32[2048,256]{1,0:T(8,128)S(1)}, f32[2048,256]{1,0:T(8,128)S(1)}, f32[224,1024]{1,0:T(8,128)S(1)}, f32[224,1024]{1,0:T(8,128)S(1)}, f32[224,1024]{1,0:T(8,128)S(1)}) custom-call(bf16[32,2048]{1,0:T(8,128)(2,1)} %tok.1, bf16[32,2048]{1,0:T(8,128)(2,1)} %grd.1, bf16[2048,896]{1,0:T(8,128)(2,1)} %gate_h.1, bf16[2048,896]{1,0:T(8,128)(2,1)} %up_h.1, ...), custom_call_target="tpu_custom_call" | custom-call | tf_op jit(solution)/shard_map/ekfac_factors/pallas_call | solution.py:656
  124.1 1.3 %copy.19 = f32[2048,256]{1,0:T(8,128)} copy(f32[2048,256]{1,0:T(8,128)S(1)} %get-tuple-element.7) | data formatting | bytes 4194304
  125.5 0.9 copy.21
  126.4 0.9 copy.22
  127.3 0.9 copy.23
  128.2 1.3 %copy.20 = f32[2048,256]{1,0:T(8,128)} copy(f32[2048,256]{1,0:T(8,128)S(1)} %get-tuple-element.8) | data formatting | bytes 4194304
  (3 shorter events, 0.0 us)

commit v3 on v2

--- a/solution.py
+++ b/solution.py
@@ -245,15 +245,13 @@
         return pl.ds(pl.multiple_of(base + UNITS * t, 32), UNITS)
 
     part_of = (pl.ds(0, 1), pl.ds(1, 2))
+    arrays_of = ((0,), (1, 2))
     own_sem, cross_sem, relay_sem = (
-        [[recv.take() for _ in (0, 1)] for _ in range(CHUNKS)] for _ in range(3)
+        [[recv.take(2) for _ in (0, 1)] for _ in range(CHUNKS)] for _ in range(3)
     )
 
     def units(part, k, q, t):
         return vw.at[part_of[part], chunk_pkgs[k][q], rows_of(t)]
-
-    def units_arrived(part, t, r):
-        arrived(vw.at[part_of[part], pl.ds(0, 2), rows_of(t)], r)
 
     def finish(k, part):
         for m in (GATE, UP) if part == 0 else (BACK,):
@@ -287,21 +285,20 @@
         lax.fori_loop(0, UNITS // 32, body, 0)
         for q in (0, 1):
             mine = units(part, k, q, tensor)
-            push(mine, mine, partner, cross_sem[k][part], "cross")
+            push(mine, mine, partner, cross_sem[k][part] + q, "cross")
         for q in (0, 1):
             mine = units(part, k, q, tensor)
-            push(mine, mine, sibling, own_sem[k][part], "own")
-
-    def relay(k, part):
-        units_arrived(part, (1 - xl) * 2 + c, cross_sem[k][part])
-        for q in (0, 1):
-            theirs = units(part, k, q, (1 - xl) * 2 + c)
-            push(theirs, theirs, sibling, relay_sem[k][part], "relay")
-
-    def slice_complete(k):
-        for part in (0, 1):
-            units_arrived(part, xl * 2 + 1 - c, own_sem[k][part])
-            units_arrived(part, (1 - xl) * 2 + 1 - c, relay_sem[k][part])
+            push(mine, mine, sibling, own_sem[k][part] + q, "own")
+
+    def relay(k, part, q):
+        theirs = units(part, k, q, (1 - xl) * 2 + c)
+        arrived(theirs, cross_sem[k][part] + q)
+        push(theirs, theirs, sibling, relay_sem[k][part] + q, "relay")
+
+    def package_ready(k, part, q):
+        p = jnp.where(q == 0, *chunk_pkgs[k])
+        for t, sem in ((xl * 2 + 1 - c, own_sem), ((1 - xl) * 2 + 1 - c, relay_sem)):
+            arrived(vw.at[part_of[part], p, rows_of(t)], sem[k][part] + q)
 
     low = e <= 3
     n_down = jnp.where(e <= 4, e, 0)
@@ -312,91 +309,100 @@
     near_y, near_z = (near_dp // 4) % 4, near_dp % 4
     my_pkg = [jnp.where(c == 0, *chunk_pkgs[k]) for k in range(CHUNKS)]
     near_pkg = [jnp.where(c == 0, *pkgs_of(k, near_y, near_z)) for k in range(CHUNKS)]
-    near_sem, near_relay = ([recv.take() for _ in range(CHUNKS)] for _ in range(2))
-    down_send, up_send, near_send = ([send.take() for _ in range(CHUNKS)] for _ in range(3))
+    near_sem, near_relay = ([recv.take(2) for _ in range(CHUNKS)] for _ in range(2))
+    down_send, up_send, near_send = ([send.take(2) for _ in range(CHUNKS)] for _ in range(3))
 
     def sized(count, most, f):
         for n in range(1, most + 1):
             pl.when(count == n)(functools.partial(f, n))
 
-    def win(p, row, n):
-        return vw.at[:, p, pl.ds(pl.multiple_of(row, PIECE), n * PIECE)]
-
-    def down_copy(k, n):
+    def win(part, p, row, n):
+        return vw.at[part_of[part], p, pl.ds(pl.multiple_of(row, PIECE), n * PIECE)]
+
+    def down_copy(k, part, n):
         return pltpu.make_async_remote_copy(
-            src_ref=win(my_pkg[k], base, n), dst_ref=win(my_pkg[k], base + 1024, n),
-            send_sem=ssem.at[down_send[k]], recv_sem=rsem.at[near_sem[k]],
+            src_ref=win(part, my_pkg[k], base, n), dst_ref=win(part, my_pkg[k], base + 1024, n),
+            send_sem=ssem.at[down_send[k] + part], recv_sem=rsem.at[near_sem[k] + part],
             device_id=below, device_id_type=MESH,
         )
 
-    def up_copy(k, n):
+    def up_copy(k, part, n):
         return pltpu.make_async_remote_copy(
-            src_ref=win(my_pkg[k], base + PIECE * e, n), dst_ref=win(my_pkg[k], 0, n),
-            send_sem=ssem.at[up_send[k]], recv_sem=rsem.at[near_sem[k]],
+            src_ref=win(part, my_pkg[k], base + PIECE * e, n), dst_ref=win(part, my_pkg[k], 0, n),
+            send_sem=ssem.at[up_send[k] + part], recv_sem=rsem.at[near_sem[k] + part],
             device_id=above, device_id_type=MESH,
         )
 
-    def near_copy(k, n):
-        ref = win(near_pkg[k], near_row, n)
+    def near_copy(k, part, n):
+        ref = win(part, near_pkg[k], near_row, n)
         return pltpu.make_async_remote_copy(
-            src_ref=ref, dst_ref=ref, send_sem=ssem.at[near_send[k]], recv_sem=rsem.at[near_relay[k]],
+            src_ref=ref, dst_ref=ref, send_sem=ssem.at[near_send[k] + part], recv_sem=rsem.at[near_relay[k] + part],
             device_id=sibling, device_id_type=MESH,
         )
 
-    def send_neighbours(k):
-        sized(n_down, 4, lambda n: down_copy(k, n).start())
-        sized(n_up, 4, lambda n: up_copy(k, n).start())
-
-    def relay_neighbours(k):
+    def pass_on(k, part):
+        for q in (0, 1):
+            relay(k, part, q)
+
+            @pl.when(c == q)
+            def _():
+                package_ready(k, part, q)
+                sized(n_down, 4, lambda n: down_copy(k, part, n).start())
+                sized(n_up, 4, lambda n: up_copy(k, part, n).start())
+
+    def relay_neighbours(k, part):
         def go(n):
-            arrived(win(near_pkg[k], near_row, n), near_sem[k])
-            near_copy(k, n).start()
+            arrived(win(part, near_pkg[k], near_row, n), near_sem[k] + part)
+            near_copy(k, part, n).start()
 
         sized(n_near, 4, go)
 
-    def neighbours_complete(k):
-        sized(n_near, 4, lambda n: arrived(win(near_pkg[k], near_row, n), near_relay[k]))
-
-    def neighbours_sent(k):
-        sized(n_down, 4, lambda n: down_copy(k, n).wait_send())
-        sized(n_up, 4, lambda n: up_copy(k, n).wait_send())
-        sized(n_near, 4, lambda n: near_copy(k, n).wait_send())
+    def units_complete(k, part):
+        package_ready(k, part, 1 - c)
+        sized(n_near, 4, lambda n: arrived(win(part, near_pkg[k], near_row, n), near_relay[k] + part))
+
+    def neighbours_sent(k, part):
+        sized(n_down, 4, lambda n: down_copy(k, part, n).wait_send())
+        sized(n_up, 4, lambda n: up_copy(k, part, n).wait_send())
+        sized(n_near, 4, lambda n: near_copy(k, part, n).wait_send())
 
     major = jnp.logical_or(e <= 2, e >= 5)
     n_cols = jnp.where(low, 7 - e, e)
     first_col = jnp.where(low, e, 0)
-    res_sem = recv.take(8)
-    res_send = send.take(24)
+    res_sem = recv.take(16)
+    res_send = send.take(48)
     pair = (tensor, tensor + 4)
 
-    def result_copy(i, r, h):
+    def result_copy(part, i, r, h):
         row = jnp.where(low, 0, PIECE * (e - 1)) + PIECE * i + 32 * r
         owner = row // UNITS
         col = jnp.where(low, 0, 8 - e) + pair[h]
         return pltpu.make_async_remote_copy(
-            src_ref=stage.at[:, i, pl.ds(32 * r, 32), pl.ds(128 * h, 128)],
+            src_ref=stage.at[part_of[part], i, pl.ds(32 * r, 32), pl.ds(128 * h, 128)],
             dst_ref=res.at[
-                :, pl.ds(pl.multiple_of(row - UNITS * owner, 32), 32), pl.ds(pl.multiple_of(128 * col, 128), 128)
+                part_of[part],
+                pl.ds(pl.multiple_of(row - UNITS * owner, 32), 32),
+                pl.ds(pl.multiple_of(128 * col, 128), 128),
             ],
-            send_sem=ssem.at[res_send + 8 * i + 2 * r + h], recv_sem=rsem.at[res_sem + col],
+            send_sem=ssem.at[res_send + 24 * part + 8 * i + 2 * r + h], recv_sem=rsem.at[res_sem + 8 * part + col],
             device_id={"dp": near_dp % 32, "tensor": owner}, device_id_type=MESH,
         )
 
-    def each_result(i, f):
+    def each_result(part, i, f):
         for h in (0, 1):
             @pl.when(pair[h] < n_cols)
             def _():
                 for r in range(4):
-                    f(result_copy(i, r, h))
-
-    def products_for_neighbour():
+                    f(result_copy(part, i, r, h))
+
+    def products_for_neighbour(part):
         def body(i, _):
             rows = pl.ds(pl.multiple_of(near_row + PIECE * i, PIECE), PIECE)
             cols_at = [
                 pl.ds(pl.multiple_of(base + PIECE * (first_col + jnp.minimum(piece, n_cols - 1)), PIECE), PIECE)
                 for piece in pair
             ]
-            for j in range(3):
+            for j in arrays_of[part]:
                 lhs = jnp.concatenate(
                     [(vw[j, p, rows].astype(F32) * wrow[p]).astype(BF) for p in range(8)], axis=1
                 )
@@ -406,7 +412,7 @@
                 stage[j, i] = lax.dot_general(
                     lhs, rhs, (((1,), (1,)), ((), ())), preferred_element_type=F32
                 ).astype(BF)
-            each_result(i, lambda copy: copy.start())
+            each_result(part, i, lambda copy: copy.start())
             return 0
 
         @pl.when(major)
@@ -415,7 +421,8 @@
 
     def products_sent():
         def body(i, _):
-            each_result(i, lambda copy: copy.wait_send())
+            for part in (0, 1):
+                each_result(part, i, lambda copy: copy.wait_send())
             return 0
 
         @pl.when(major)
@@ -499,7 +506,7 @@
     has_early, has_late = split_row > 0, split_row < UNITS
     blk_out = (hid_o, gg_o, ug_o)
 
-    def block_cov():
+    def block_cov(part):
         row = lax.broadcasted_iota(jnp.int32, (UNITS, 256), 0)
 
         def body(g, _):
@@ -512,12 +519,12 @@
 
             @pl.when(jnp.logical_and(has_late, jnp.logical_or(low, 2 * g <= 6 - e)))
             def _():
-                for j in range(3):
+                for j in arrays_of[part]:
                     blk_out[j][:, pl.ds(k, 256)] = product(j, 1024)
 
             @pl.when(jnp.logical_and(has_early, jnp.logical_or(jnp.logical_not(low), 2 * g + 1 >= 8 - e)))
             def _():
-                for j in range(3):
+                for j in arrays_of[part]:
                     blk_out[j][:, pl.ds(k, 256)] = jnp.where(
                         row < split_row, product(j, 0), blk_out[j][:, pl.ds(k, 256)]
                     )
@@ -526,7 +533,7 @@
 
         lax.fori_loop(0, 4, body, 0)
 
-    def products_from_neighbour():
+    def products_from_neighbour(part):
         row = lax.broadcasted_iota(jnp.int32, (UNITS, 128), 0)
         minor_early = jnp.logical_and(jnp.logical_and(low, e >= 1), has_early)
         minor_late = jnp.logical_and(jnp.logical_and(jnp.logical_not(low), e <= 6), has_late)
@@ -537,10 +544,10 @@
         to_row = jnp.where(low, split_row, UNITS)
 
         def body(col, _):
-            sized(bands, 7, lambda n: arrived(res.at[:, pl.ds(0, 32 * n), pl.ds(0, 128)], res_sem + col))
+            sized(bands, 7, lambda n: arrived(res.at[part_of[part], pl.ds(0, 32 * n), pl.ds(0, 128)], res_sem + 8 * part + col))
             at = pl.ds(pl.multiple_of(col * 128, 128), 128)
             here_too = jnp.logical_and(row >= from_row, row < to_row)
-            for j in range(3):
+            for j in arrays_of[part]:
                 blk_out[j][:, at] = jnp.where(here_too, res[j, :, at].astype(F32), blk_out[j][:, at])
             return 0
 
@@ -580,16 +587,14 @@
     combine(2, BACK)
     finish(1, 0)
     finish(2, 0)
-    relay(0, 0)
-    relay(0, 1)
+    pass_on(0, 0)
     far_packages(0)
     send_cols(0)
     project(3, GATE)
     project(3, UP)
     combine(3, GATE)
     combine(3, UP)
-    slice_complete(0)
-    send_neighbours(0)
+    pass_on(0, 1)
     finish(1, 1)
     finish(2, 1)
     far_packages(1)
@@ -597,30 +602,35 @@
     project(3, BACK)
     combine(3, BACK)
     finish(3, 0)
-    for k in (1, 2):
-        relay(k, 0)
-    for k in (1, 2):
-        relay(k, 1)
-        slice_complete(k)
-        send_neighbours(k)
-    relay_neighbours(0)
+    pass_on(1, 0)
+    pass_on(2, 0)
+    pass_on(1, 1)
+    pass_on(2, 1)
+    relay_neighbours(0, 0)
+    relay_neighbours(0, 1)
     finish(3, 1)
     cols_complete(0)
     full_cov(0)
-    relay(3, 0)
-    relay(3, 1)
-    slice_complete(3)
-    send_neighbours(3)
-    relay_neighbours(1)
+    pass_on(3, 0)
+    relay_neighbours(1, 0)
+    relay_neighbours(2, 0)
+    pass_on(3, 1)
+    relay_neighbours(3, 0)
+    relay_neighbours(1, 1)
+    relay_neighbours(2, 1)
+    for k in range(CHUNKS):
+        units_complete(k, 0)
+    products_for_neighbour(0)
+    block_cov(0)
+    relay_neighbours(3, 1)
+    for k in range(CHUNKS):
+        units_complete(k, 1)
+    products_for_neighbour(1)
     cols_complete(1)
     full_cov(1)
-    relay_neighbours(2)
-    relay_neighbours(3)
-    for k in range(CHUNKS):
-        neighbours_complete(k)
-    products_for_neighbour()
-    block_cov()
-    products_from_neighbour()
+    block_cov(1)
+    products_from_neighbour(0)
+    products_from_neighbour(1)
     for copy in slot_sent:
         copy.wait_send()
     group_sent("twin", xt.at[0, 0, pl.ds(0, 64)])
@@ -633,14 +643,24 @@
     group_sent("own", sb)
     group_sent("relay", sb)
     for k in range(CHUNKS):
-        neighbours_sent(k)
+        for part in (0, 1):
+            neighbours_sent(k, part)
     for a in (0, 1):
         cols_sent(a)
     products_sent()
     assert (send.used, recv.used, here.used) == (N_SEND, N_RECV, N_LOCAL)
 
 
-N_SEND, N_RECV, N_LOCAL = 52, 102, 9
+N_SEND, N_RECV, N_LOCAL = 88, 142, 9
+
+
+def write_out(*refs):
+    sources, targets, sems = refs[:5], refs[5:10], refs[10]
+    copies = [pltpu.make_async_copy(a, b, sems.at[i]) for i, (a, b) in enumerate(zip(sources, targets))]
+    for copy in copies:
+        copy.start()
+    for copy in copies:
+        copy.wait()
 
 
 def local(tokens, out_grad, gate_weight, up_weight, down_weight, pocket_ids):
@@ -653,7 +673,7 @@
     )
     any_spec = pl.BlockSpec(memory_space=pl.ANY)
     vmem = pl.BlockSpec(memory_space=pltpu.VMEM)
-    return pl.pallas_call(
+    factors = pl.pallas_call(
         kernel,
         out_shape=[
             pltpu.VMEM((2048, 256), F32),
@@ -691,6 +711,15 @@
         ),
         name="ekfac_factors",
     )(tokens, out_grad, gate_weight, up_weight, down_weight, ids)
+    return pl.pallas_call(
+        write_out,
+        out_shape=[jax.ShapeDtypeStruct(factor.shape, F32) for factor in factors],
+        in_specs=[vmem] * 5,
+        out_specs=[any_spec] * 5,
+        scratch_shapes=[pltpu.SemaphoreType.DMA((5,))],
+        compiler_params=pltpu.CompilerParams(vmem_limit_bytes=4 * MIB),
+        name="write_factors",
+    )(*(pltpu.with_memory_space_constraint(factor, pltpu.VMEM) for factor in factors))
 
 
 def solution(mesh):

time: 130 us -> 122 us (0.938)
  local copies, waits for them, and re-layouts: 6.4 us -> 1 us
  Pallas kernels: 122 us -> 119 us
    pallas_call x1, Pallas kernels: 122 us -> 116 us  [local(): pl.pallas_call(kernel, out_shape=[pltpu.VMEM((2048, 256), F32), pltpu.VME...]
    unnamed x5 -> x0, local copies, waits for them, and re-layouts: 5.41 us -> none
    pallas_call x0 -> x1, Pallas kernels: none -> 2.9 us  [local(): pl.pallas_call(write_out, out_shape=[jax.ShapeDtypeStruct(factor.shape, F...]
where the time goes in v3:
time: 122 us
  Pallas kernels  119 us (98%)
    pallas_call x1, Pallas kernels, local(): pl.pallas_call(kernel, out_shape=[pltpu.VMEM((2048, 256), F32), pltpu.VME...  116 us
    pallas_call x1, Pallas kernels, local(): pl.pallas_call(write_out, out_shape=[jax.ShapeDtypeStruct(factor.shape, F...  2.9 us

profile of v3, /device:TPU:15, one launch (start us, length us, event | category | flops | bytes accessed | tf_op | source)
XLA Modules:
  0.0 121.8 jit_solution(11528418526739103924)
XLA Ops:
  0.6 0.8 reshape.19
  1.5 0.1 reshape.20
  1.6 0.1 reshape.21
  1.7 0.6 pad_add_fusion.ids_ref
  2.3 116.4 %ekfac_factors.1 = (f32[2048,256]{1,0:T(8,128)S(1)}, f32[2048,256]{1,0:T(8,128)S(1)}, f32[224,1024]{1,0:T(8,128)S(1)}, f32[224,1024]{1,0:T(8,128)S(1)}, f32[224,1024]{1,0:T(8,128)S(1)}) custom-call(bf16[32,2048]{1,0:T(8,128)(2,1)} %tok.1, bf16[32,2048]{1,0:T(8,128)(2,1)} %grd.1, bf16[2048,896]{1,0:T(8,128)(2,1)} %gate_h.1, bf16[2048,896]{1,0:T(8,128)(2,1)} %up_h.1, ...), custom_call_target="tpu_custom_call" | custom-call | tf_op jit(solution)/shard_map/ekfac_factors/pallas_call | solution.py:676
  118.7 2.9 %write_factors.1 = (f32[2048,256]{1,0:T(8,128)}, f32[2048,256]{1,0:T(8,128)}, f32[224,1024]{1,0:T(8,128)}, f32[224,1024]{1,0:T(8,128)}, f32[224,1024]{1,0:T(8,128)}) custom-call(f32[2048,256]{1,0:T(8,128)S(1)} %get-tuple-element.10.refs_0_, f32[2048,256]{1,0:T(8,128)S(1)} %get-tuple-element.11.refs_1_, f32[224,1024]{1,0:T(8,128)S(1)} %get-tuple-element.12.refs_2_, ...), custom_call_target="tpu_custom_call" | custom-call | tf_op jit(solution)/shard_map/write_factors/pallas_call | solution.py:714
  (3 shorter events, 0.0 us)

commit v4 on v3

--- a/solution.py
+++ b/solution.py
@@ -105,9 +105,22 @@
             member = (ids == k).astype(F32)
             count = jnp.sum(jnp.sum(member, axis=1, keepdims=True), axis=0, keepdims=True)
             weights = weights + member * (1.0 / (POCKETS * count))
+        band = lax.broadcasted_iota(jnp.int32, (8, 128), 1) // 16
+
+        def picked(start, at):
+            return jnp.where(band == at, pltpu.roll(weights, (16 * (at - start)) % 128, 1), 0.0)
+
+        halves = jnp.zeros((4, 128), F32)
+        for at in range(8):
+            h = at // 4
+            halves = halves + picked(2 * (at % 4), at)[4 * h : 4 * h + 4]
+        packages = [halves]
+        for k in range(4):
+            packages.append(sum(picked(2 * k + 1, at)[at : at + 1] for at in range(8)))
+        ordered = jnp.concatenate(packages, axis=0)
         for p in range(8):
-            wrow[p] = weights[p : p + 1]
-        wcol[...] = weights.T
+            wrow[p] = ordered[p : p + 1]
+        wcol[...] = ordered.T
 
     pocket_weights()
 
@@ -664,13 +677,7 @@
 
 
 def local(tokens, out_grad, gate_weight, up_weight, down_weight, pocket_ids):
-    ids = pocket_ids.reshape(2, 4, 4, 2, 16)
-    ids = jnp.concatenate(
-        [
-            ids[:, :, :, 0].transpose(1, 0, 2, 3).reshape(4, 128),
-            ids[:, :, :, 1].transpose(2, 0, 1, 3).reshape(4, 128),
-        ]
-    )
+    ids = pocket_ids.reshape(8, 128)
     any_spec = pl.BlockSpec(memory_space=pl.ANY)
     vmem = pl.BlockSpec(memory_space=pltpu.VMEM)
     factors = pl.pallas_call(

time: 122 us -> 120 us (0.984)
  no operation moved by 1% of the time
where the time goes in v4:
time: 120 us
  Pallas kernels  119 us (99%)
    pallas_call x1, Pallas kernels, local(): pl.pallas_call(kernel, out_shape=[pltpu.VMEM((2048, 256), F32), pltpu.VME...  117 us
    pallas_call x1, Pallas kernels, local(): pl.pallas_call(write_out, out_shape=[jax.ShapeDtypeStruct(factor.shape, F...  2.9 us

profile of v4, /device:TPU:15, one launch (start us, length us, event | category | flops | bytes accessed | tf_op | source)
XLA Modules:
  0.0 120.3 jit_solution(2238194341376261343)
XLA Ops:
  0.6 116.6 %ekfac_factors.1 = (f32[2048,256]{1,0:T(8,128)S(1)}, f32[2048,256]{1,0:T(8,128)S(1)}, f32[224,1024]{1,0:T(8,128)S(1)}, f32[224,1024]{1,0:T(8,128)S(1)}, f32[224,1024]{1,0:T(8,128)S(1)}) custom-call(bf16[32,2048]{1,0:T(8,128)(2,1)} %tok.1, bf16[32,2048]{1,0:T(8,128)(2,1)} %grd.1, bf16[2048,896]{1,0:T(8,128)(2,1)} %gate_h.1, bf16[2048,896]{1,0:T(8,128)(2,1)} %up_h.1, ...), custom_call_target="tpu_custom_call" | custom-call | tf_op jit(solution)/shard_map/ekfac_factors/pallas_call | solution.py:683
  117.2 2.9 %write_factors.1 = (f32[2048,256]{1,0:T(8,128)}, f32[2048,256]{1,0:T(8,128)}, f32[224,1024]{1,0:T(8,128)}, f32[224,1024]{1,0:T(8,128)}, f32[224,1024]{1,0:T(8,128)}) custom-call(f32[2048,256]{1,0:T(8,128)S(1)} %get-tuple-element.10.refs_0_, f32[2048,256]{1,0:T(8,128)S(1)} %get-tuple-element.11.refs_1_, f32[224,1024]{1,0:T(8,128)S(1)} %get-tuple-element.12.refs_2_, ...), custom_call_target="tpu_custom_call" | custom-call | tf_op jit(solution)/shard_map/write_factors/pallas_call | solution.py:721

commit v5 on v4

--- a/solution.py
+++ b/solution.py
@@ -622,8 +622,6 @@
     relay_neighbours(0, 0)
     relay_neighbours(0, 1)
     finish(3, 1)
-    cols_complete(0)
-    full_cov(0)
     pass_on(3, 0)
     relay_neighbours(1, 0)
     relay_neighbours(2, 0)
@@ -631,6 +629,8 @@
     relay_neighbours(3, 0)
     relay_neighbours(1, 1)
     relay_neighbours(2, 1)
+    cols_complete(0)
+    full_cov(0)
     for k in range(CHUNKS):
         units_complete(k, 0)
     products_for_neighbour(0)

time: 120 us -> 120 us (level)
  no operation moved by 1% of the time
where the time goes in v5:
time: 120 us
  Pallas kernels  119 us (99%)
    pallas_call x1, Pallas kernels, local(): pl.pallas_call(kernel, out_shape=[pltpu.VMEM((2048, 256), F32), pltpu.VME...  116 us
    pallas_call x1, Pallas kernels, local(): pl.pallas_call(write_out, out_shape=[jax.ShapeDtypeStruct(factor.shape, F...  2.9 us

profile of v5, /device:TPU:15, one launch (start us, length us, event | category | flops | bytes accessed | tf_op | source)
XLA Modules:
  0.0 119.9 jit_solution(7631850500500447966)
XLA Ops:
  0.6 116.2 %ekfac_factors.1 = (f32[2048,256]{1,0:T(8,128)S(1)}, f32[2048,256]{1,0:T(8,128)S(1)}, f32[224,1024]{1,0:T(8,128)S(1)}, f32[224,1024]{1,0:T(8,128)S(1)}, f32[224,1024]{1,0:T(8,128)S(1)}) custom-call(bf16[32,2048]{1,0:T(8,128)(2,1)} %tok.1, bf16[32,2048]{1,0:T(8,128)(2,1)} %grd.1, bf16[2048,896]{1,0:T(8,128)(2,1)} %gate_h.1, bf16[2048,896]{1,0:T(8,128)(2,1)} %up_h.1, ...), custom_call_target="tpu_custom_call" | custom-call | tf_op jit(solution)/shard_map/ekfac_factors/pallas_call | solution.py:683
  116.8 2.9 %write_factors.1 = (f32[2048,256]{1,0:T(8,128)}, f32[2048,256]{1,0:T(8,128)}, f32[224,1024]{1,0:T(8,128)}, f32[224,1024]{1,0:T(8,128)}, f32[224,1024]{1,0:T(8,128)}) custom-call(f32[2048,256]{1,0:T(8,128)S(1)} %get-tuple-element.10.refs_0_, f32[2048,256]{1,0:T(8,128)S(1)} %get-tuple-element.11.refs_1_, f32[224,1024]{1,0:T(8,128)S(1)} %get-tuple-element.12.refs_2_, ...), custom_call_target="tpu_custom_call" | custom-call | tf_op jit(solution)/shard_map/write_factors/pallas_call | solution.py:721

commit v6 on v5

--- a/solution.py
+++ b/solution.py
@@ -585,6 +585,7 @@
     finish(0, 0)
     forward_packages(0)
     project(1, GATE)
+    finish(0, 1)
     project(1, UP)
     combine(1, GATE)
     project(2, GATE)
@@ -592,7 +593,6 @@
     project(2, UP)
     combine(2, GATE)
     combine(2, UP)
-    finish(0, 1)
     forward_packages(1)
     project(1, BACK)
     project(2, BACK)

time: 120 us -> 117 us (0.975)
  Pallas kernels: 119 us -> 116 us
    pallas_call x1, Pallas kernels: 116 us -> 113 us  [local(): pl.pallas_call(kernel, out_shape=[pltpu.VMEM((2048, 256), F32), pltpu.VME...]
where the time goes in v6:
time: 117 us
  Pallas kernels  116 us (99%)
    pallas_call x1, Pallas kernels, local(): pl.pallas_call(kernel, out_shape=[pltpu.VMEM((2048, 256), F32), pltpu.VME...  113 us
    pallas_call x1, Pallas kernels, local(): pl.pallas_call(write_out, out_shape=[jax.ShapeDtypeStruct(factor.shape, F...  2.9 us

profile of v6, /device:TPU:15, one launch (start us, length us, event | category | flops | bytes accessed | tf_op | source)
XLA Modules:
  0.0 117.2 jit_solution(7291523709820092685)
XLA Ops:
  0.6 113.4 %ekfac_factors.1 = (f32[2048,256]{1,0:T(8,128)S(1)}, f32[2048,256]{1,0:T(8,128)S(1)}, f32[224,1024]{1,0:T(8,128)S(1)}, f32[224,1024]{1,0:T(8,128)S(1)}, f32[224,1024]{1,0:T(8,128)S(1)}) custom-call(bf16[32,2048]{1,0:T(8,128)(2,1)} %tok.1, bf16[32,2048]{1,0:T(8,128)(2,1)} %grd.1, bf16[2048,896]{1,0:T(8,128)(2,1)} %gate_h.1, bf16[2048,896]{1,0:T(8,128)(2,1)} %up_h.1, ...), custom_call_target="tpu_custom_call" | custom-call | tf_op jit(solution)/shard_map/ekfac_factors/pallas_call | solution.py:683
  114.1 2.9 %write_factors.1 = (f32[2048,256]{1,0:T(8,128)}, f32[2048,256]{1,0:T(8,128)}, f32[224,1024]{1,0:T(8,128)}, f32[224,1024]{1,0:T(8,128)}, f32[224,1024]{1,0:T(8,128)}) custom-call(f32[2048,256]{1,0:T(8,128)S(1)} %get-tuple-element.10.refs_0_, f32[2048,256]{1,0:T(8,128)S(1)} %get-tuple-element.11.refs_1_, f32[224,1024]{1,0:T(8,128)S(1)} %get-tuple-element.12.refs_2_, ...), custom_call_target="tpu_custom_call" | custom-call | tf_op jit(solution)/shard_map/write_factors/pallas_call | solution.py:721
